TPU v7x, 32 devices: a whole 2x2x4 slice. The times are simulated.
32 devices in a mesh: rep: 4 (over z), member: 8 (over y, x, core).
Axes of the slice: x: 2, y: 2, z: 4, core: 2. Of those that a mesh axis runs over, the one named last changes fastest.
Arguments:
- acts: bfloat16 [512, 2, 100, 128], P(('rep', 'member')), may hold values from -6 to 6
- cotangent: bfloat16 [512, 2, 100, 128], P(('rep', 'member')), may hold values from -6 to 6
- routes: int32 [512, 2], P(('rep', 'member')), may hold values from 0 to 7, all different within a row; in each aligned block of 16 rows (0 to 15, 16 to 31, ...) at most 8 rows name the same one
- w_first: bfloat16 [8, 1152, 128], P('member'), may hold values from -0.1875 to 0.1875
- w_second: bfloat16 [8, 1152, 128], P('member'), may hold values from -0.1875 to 0.1875
- b_first: float32 [8, 128], P('member'), may hold values from -3 to 3
- b_second: float32 [8, 128], P('member'), may hold values from -3 to 3
Outputs:
- out_acts: bfloat16 [512, 2, 100, 128], P(('rep', 'member'))
- grad_acts: bfloat16 [512, 2, 100, 128], P(('rep', 'member'))
- grad_w_first: float32 [8, 1152, 128], P('member')
- grad_w_second: float32 [8, 1152, 128], P('member')
- grad_b_first: float32 [8, 128], P('member')
- grad_b_second: float32 [8, 128], P('member')
Inputs may be any that keep to these rules, and one draw needn't show every extreme that they name: `routes`: the two members of a state differ. Among the 16 states of one device no member is named more than 8 times, and in some device one member is named exactly 8 times. Every member is named by some state.
All inputs are finite; a program needn't handle non-finite values.
Results may differ from a plain program's by a relative error of at most 0.007.
Values may be sent and summed in bfloat16 or wider, within the bound.
A program may use at most 64 MiB of HBM per device.

v0:
```python
import functools

import jax
import jax.numpy as jnp
from jax import lax
from jax.experimental import pallas as pl
from jax.experimental.pallas import tpu as pltpu
from jax.sharding import PartitionSpec as P

BOARD = 10


def flipped(weight):
    channels = weight.shape[-1]
    stacked = weight.reshape(weight.shape[:-2] + (9, channels, channels))
    reversed_taps = jnp.flip(stacked, axis=-3)
    return jnp.swapaxes(reversed_taps, -1, -2).reshape(weight.shape)


def silu_slope(pre_act):
    sigmoid_vals = jax.nn.sigmoid(pre_act)
    return sigmoid_vals * (1.0 + pre_act * (1.0 - sigmoid_vals))


def board_conv(values, weight):
    count = values.shape[0]
    channels = values.shape[-1]
    side = BOARD
    boards = values.reshape(count, side, side, channels)
    kernel = weight.reshape(3, 3, channels, channels)
    result = lax.conv_general_dilated(
        boards,
        kernel,
        (1, 1),
        ((1, 1), (1, 1)),
        dimension_numbers=("NHWC", "HWIO", "NHWC"),
        preferred_element_type=jnp.float32,
    )
    return result.reshape(count, side * side, channels)


def weight_conv(values, grads):
    count = values.shape[0]
    channels = values.shape[-1]
    side = BOARD
    boards = values.reshape(count, side, side, channels)
    grad_boards = grads.reshape(count, side, side, channels)
    result = lax.conv_general_dilated(
        boards,
        grad_boards,
        (1, 1),
        ((1, 1), (1, 1)),
        dimension_numbers=("CHWN", "IHWO", "NHWC"),
        preferred_element_type=jnp.float32,
    )
    return jnp.transpose(result, (1, 2, 0, 3)).reshape(9 * channels, channels)


def shards(acts, cotangent, routes, w_first, w_second, b_first, b_second):
    per_owner = w_first.shape[0]
    owners = lax.axis_size("member")
    members_all = owners * per_owner
    capacity = max(2, 4 * routes.shape[0] // members_all)
    channels = acts.shape[-1]
    cell_count = acts.shape[-2]
    member_ids = routes.reshape(-1)
    onehot = (member_ids[:, None] == jnp.arange(members_all, dtype=jnp.int32)[None, :]).astype(
        jnp.int32
    )
    order = jnp.arange(member_ids.shape[0], dtype=jnp.int32)
    earlier = jnp.sum((order[:, None] > order[None, :])[:, :, None] * onehot[None], axis=1)
    slot_index = jnp.sum(earlier * onehot, axis=1)
    target = member_ids * capacity + slot_index
    dispatch = (
        jnp.arange(members_all * capacity, dtype=jnp.int32)[:, None] == target[None, :]
    ).astype(jnp.bfloat16)

    def scatter_rows(values):
        flattened = values.reshape(-1, cell_count * channels)
        placed = jnp.dot(dispatch, flattened, preferred_element_type=jnp.float32).astype(
            jnp.bfloat16
        )
        return placed.reshape(members_all, capacity, cell_count, channels)

    def gather_rows(values):
        flattened = values.reshape(members_all * capacity, cell_count * channels)
        picked = jnp.dot(dispatch.T, flattened, preferred_element_type=jnp.float32).astype(
            jnp.bfloat16
        )
        return picked.reshape(acts.shape)

    def to_local(received):
        grouped = received.reshape(owners, per_owner, capacity, cell_count, channels)
        return jnp.swapaxes(grouped, 0, 1).reshape(
            per_owner, owners * capacity, cell_count, channels
        )

    def from_local(values):
        grouped = values.reshape(per_owner, owners, capacity, cell_count, channels)
        return jnp.swapaxes(grouped, 0, 1).reshape(members_all, capacity, cell_count, channels)

    send_acts = scatter_rows(acts)
    send_grads = scatter_rows(cotangent)
    recv_acts, recv_grads = (
        lax.all_to_all(send_acts, "member", split_axis=0, concat_axis=0, tiled=True),
        lax.all_to_all(send_grads, "member", split_axis=0, concat_axis=0, tiled=True),
    )
    inputs = to_local(recv_acts)
    upstream = to_local(recv_grads)
    owned = 0
    pre_one = board_conv(inputs[owned], w_first[owned]) + b_first[owned][None, None, :]
    hidden_one = jax.nn.silu(pre_one).astype(jnp.bfloat16)
    result_one = (
        inputs[owned].astype(jnp.float32)
        + board_conv(hidden_one, w_second[owned])
        + b_second[owned][None, None, :]
    ).astype(jnp.bfloat16)
    pre_list = [pre_one]
    hidden_list = [hidden_one]
    result_list = [result_one]
    result = jnp.stack(result_list)
    owned = 0
    upstream_one = upstream[owned]
    grad_two_list = [weight_conv(hidden_list[owned], upstream_one)]
    bias_two_list = [jnp.sum(upstream_one.astype(jnp.float32), axis=(0, 1))]
    hidden_grad = board_conv(upstream_one, flipped(w_second[owned]))
    pre_grad = (hidden_grad * silu_slope(pre_list[owned])).astype(jnp.bfloat16)
    grad_one_list = [weight_conv(inputs[owned], pre_grad)]
    bias_one_list = [jnp.sum(pre_grad.astype(jnp.float32), axis=(0, 1))]
    input_list = [
        (upstream_one.astype(jnp.float32) + board_conv(pre_grad, flipped(w_first[owned]))).astype(
            jnp.bfloat16
        )
    ]
    input_grad = jnp.stack(input_list)
    grad_one = jnp.stack(grad_one_list)
    grad_two = jnp.stack(grad_two_list)
    bias_one = jnp.stack(bias_one_list)
    bias_two = jnp.stack(bias_two_list)
    back_out, back_in = (
        lax.all_to_all(from_local(result), "member", split_axis=0, concat_axis=0, tiled=True),
        lax.all_to_all(from_local(input_grad), "member", split_axis=0, concat_axis=0, tiled=True),
    )
    totals = lax.psum((grad_one, grad_two, bias_one, bias_two), "rep")
    return (gather_rows(back_out), gather_rows(back_in), totals[0], totals[1], totals[2], totals[3])


SLOTS = 8
SIDE = BOARD + 2
CELLS = BOARD * BOARD
ROWS = CELLS * SLOTS
LINE = BOARD * SLOTS
TAIL = 64


def inner(line):
    return ((line + 1) * SIDE + 1) * SLOTS


def fill_patches(board_ref, patch_ref, channels):
    for tap in range(9):
        down, right = tap // 3, tap % 3
        for line in range(BOARD):
            start = ((line + down) * SIDE + right) * SLOTS
            patch_ref[line * LINE : (line + 1) * LINE, tap * channels : (tap + 1) * channels] = (
                board_ref[start : start + LINE, :].astype(jnp.bfloat16)
            )


def flipped_wide(weight_ref, base, channels):
    return jnp.concatenate(
        [
            weight_ref[base + (8 - tap) * channels : base + (9 - tap) * channels, :]
            for tap in range(9)
        ],
        axis=1,
    )


def tower_kernel(extra, slots_ref, acts_ref, cot_ref, weight_ref, *rest):
    rest = rest[extra:]
    (out_ref, back_ref, grads_ref, xs, gs, hs, ps, px, ph, pq, slope, flat_out, flat_back, stage, sems) = rest
    channels = weight_ref.shape[-1]
    taps = 9 * channels
    f32, bf16 = jnp.float32, jnp.bfloat16
    count = slots_ref[SLOTS]
    for ref in (xs, gs, hs, ps):
        ref[...] = jnp.zeros_like(ref)
    for slot in range(SLOTS):

        @pl.when(slot < count)
        def _():
            row = slots_ref[slot]
            for src, dst in ((acts_ref, xs), (cot_ref, gs)):
                board = src[row].astype(f32)
                for line in range(BOARD):
                    dst[pl.ds(inner(line) + slot, BOARD, stride=SLOTS), :] = board[
                        line * BOARD : (line + 1) * BOARD
                    ]

    def bias(at):
        return (
            weight_ref[2 * taps : 2 * taps + 16, :].astype(f32)[at : at + 3].sum(axis=0, keepdims=True)
        )

    def wide(lhs, rhs):
        return lax.dot_general(lhs, rhs, (((1,), (1,)), ((), ())), preferred_element_type=f32)

    def send_rows(which, flat, ref):
        for slot in range(SLOTS):

            @pl.when(slot < count)
            def _():
                stage[which * SLOTS + slot] = flat[pl.ds(slot, CELLS, stride=SLOTS), :].astype(bf16)
                pltpu.make_async_copy(
                    stage.at[which * SLOTS + slot],
                    ref.at[slots_ref[slot]],
                    sems.at[which * SLOTS + slot],
                ).start()

    fill_patches(xs, px, channels)
    pre = jnp.dot(px[...], weight_ref[:taps, :], preferred_element_type=f32) + bias(0)
    fill_patches(gs, pq, channels)
    hidden_grad = wide(pq[...], flipped_wide(weight_ref, taps, channels))
    gate = 0.5 * jnp.tanh(0.5 * pre) + 0.5
    slope[...] = hidden_grad * (gate * (1.0 + pre * (1.0 - gate)))
    hidden = (pre * gate).astype(bf16).astype(f32)
    for line in range(BOARD):
        hs[inner(line) : inner(line) + LINE, :] = hidden[line * LINE : (line + 1) * LINE]
    fill_patches(hs, ph, channels)

    flat_out[...] = jnp.dot(ph[...], weight_ref[taps : 2 * taps, :], preferred_element_type=f32) + bias(3)
    for line in range(BOARD):
        flat_out[line * LINE : (line + 1) * LINE, :] += xs[inner(line) : inner(line) + LINE, :]

    def weight_grad(grad, patch_ref, base):
        turned = wide_grad(grad, patch_ref)
        for tap in range(9):
            grads_ref[base + tap * channels : base + (tap + 1) * channels, :] = turned[
                :, tap * channels : (tap + 1) * channels
            ].astype(bf16)

    def wide_grad(grad, patch_ref):
        return jnp.dot(grad.T.astype(bf16), patch_ref[...], preferred_element_type=f32)

    upstream = jnp.concatenate(
        [gs[inner(line) : inner(line) + LINE, :] for line in range(BOARD)], axis=0
    )
    weight_grad(upstream, ph, taps)
    bias_two = jnp.sum(upstream, axis=0, keepdims=True)

    pre_grad = slope[...].astype(bf16).astype(f32)
    for line in range(BOARD):
        ps[inner(line) : inner(line) + LINE, :] = pre_grad[line * LINE : (line + 1) * LINE]
    fill_patches(ps, pq, channels)
    bias_one = jnp.sum(pre_grad, axis=0, keepdims=True)
    flat_back[...] = wide(pq[...], flipped_wide(weight_ref, 0, channels))
    for line in range(BOARD):
        flat_back[line * LINE : (line + 1) * LINE, :] += gs[inner(line) : inner(line) + LINE, :]
    weight_grad(pre_grad, px, 0)

    place = lax.broadcasted_iota(jnp.int32, (TAIL, channels), 0)
    tail = jnp.zeros((TAIL, channels), f32)
    for at, value in ((0, bias_one), (2, bias_two)):
        high = value.astype(bf16).astype(f32)
        tail = jnp.where(place == at, high, tail)
        tail = jnp.where(place == at + 1, value - high, tail)
    grads_ref[2 * taps :, :] = tail.astype(bf16)
    send_rows(0, flat_out, out_ref)
    send_rows(1, flat_back, back_ref)

    for which, ref in ((0, out_ref), (1, back_ref)):
        for slot in range(SLOTS):

            @pl.when(slot < count)
            def _():
                pltpu.make_async_copy(
                    stage.at[which * SLOTS + slot],
                    ref.at[slots_ref[slot]],
                    sems.at[which * SLOTS + slot],
                ).wait()


def tower(slots, acts, cotangent, weight, previous, after):
    channels = acts.shape[-1]
    taps = 9 * channels
    first = previous is None
    extra = (0 if first else 2) + len(after)
    vmem = pl.BlockSpec(memory_space=pltpu.VMEM)
    anywhere = pl.BlockSpec(memory_space=pl.ANY)
    rows_shape = jax.ShapeDtypeStruct(acts.shape, acts.dtype)
    board = pltpu.VMEM((SIDE * SIDE * SLOTS, channels), jnp.float32)
    patch = pltpu.VMEM((ROWS, taps), jnp.bfloat16)
    square = pltpu.VMEM((ROWS, channels), jnp.float32)
    flops = 12 * ROWS * taps * channels
    return pl.pallas_call(
        functools.partial(tower_kernel, extra),
        out_shape=(
            rows_shape,
            rows_shape,
            jax.ShapeDtypeStruct((2 * taps + TAIL, channels), jnp.bfloat16),
        ),
        in_specs=[pl.BlockSpec(memory_space=pltpu.SMEM), vmem, vmem, vmem]
        + [anywhere] * extra,
        out_specs=(anywhere, anywhere, vmem),
        scratch_shapes=[board] * 4
        + [patch] * 3
        + [square] * 3
        + [
            pltpu.VMEM((2 * SLOTS, CELLS, channels), jnp.bfloat16),
            pltpu.SemaphoreType.DMA((2 * SLOTS,)),
        ],
        input_output_aliases={} if first else {4: 0, 5: 1},
        compiler_params=pltpu.CompilerParams(vmem_limit_bytes=40 * 1024 * 1024),
        cost_estimate=pl.CostEstimate(flops=6 * flops, bytes_accessed=4000000, transcendentals=ROWS * channels),
        name="tower",
    )(slots, acts, cotangent, weight, *(() if first else previous), *after)


def parts_of(value):
    high = lax.reduce_precision(value, 8, 7)
    middle = lax.reduce_precision(value - high, 8, 7)
    return [high, middle, value - high - middle]


def at_home(acts, cotangent, routes, w_first, w_second, b_first, b_second):
    owners = lax.axis_size("member")
    copies = lax.axis_size("rep")
    channels = acts.shape[-1]
    taps = 9 * channels
    me = lax.axis_index("member")
    member_ids = routes.reshape(-1)
    total = member_ids.shape[0]
    named = member_ids[None, :] == jnp.arange(owners, dtype=jnp.int32)[:, None]
    counts = jnp.sum(named.astype(jnp.int32), axis=1)
    order = jnp.arange(total, dtype=jnp.int32)
    before = (order[:, None] > order[None, :]) & named[:, None, :]
    place = jnp.sum(before.astype(jnp.int32), axis=2)
    hit = named[:, None, :] & (
        place[:, None, :] == jnp.arange(SLOTS, dtype=jnp.int32)[None, :, None]
    )
    rows = jnp.sum(jnp.where(hit, jnp.arange(total, dtype=jnp.int32)[None, None, :], 0), axis=2)
    table = jnp.concatenate([rows, counts[:, None]], axis=1)

    x = acts.reshape((total,) + acts.shape[2:])
    g = cotangent.reshape((total,) + acts.shape[2:])
    pieces = parts_of(b_first) + parts_of(b_second)
    bias_tile = jnp.concatenate(
        [piece.astype(jnp.bfloat16) for piece in pieces]
        + [jnp.zeros((10, channels), jnp.bfloat16)],
        axis=0,
    )
    own = jnp.concatenate([w_first[0], w_second[0], lax.optimization_barrier(bias_tile)], axis=0)

    def swap(value, offset, axis="member"):
        size = lax.axis_size(axis)
        return lax.ppermute(value, axis, [(i, i ^ offset) for i in range(size)])

    chips = owners // 2
    same = [own] + [swap(own, 2 * step) for step in range(1, chips)]
    other = [swap(value, 1) for value in same]
    previous = None
    summed = None
    after = ()
    totals = []
    held = []
    last = None
    for step in range(chips):
        made = {}
        order = (0, 1) if step == 0 else (1, 0)
        for side in order:
            weight = (same, other)[side][step]
            member = me ^ (2 * step + side)
            slots = lax.dynamic_index_in_dim(table, member, 0, keepdims=False)
            out, back, grads = tower(slots, x, g, weight, previous, after)
            after = ()
            previous = (out, back)
            made[side] = grads
        pair = made[0].astype(jnp.float32) + swap(made[1], 1).astype(jnp.float32)
        if step == 0:
            totals.append(pair)
        elif step == chips - 1:
            last = pair
        else:
            narrow = pair.astype(jnp.bfloat16)
            totals.append(swap(narrow, 2 * step).astype(jnp.float32))
            held.append(narrow)
        if held:
            after = (held.pop(),)

    rep = lax.axis_index("rep")

    def scattered(value):
        chunks = value.reshape(copies, value.shape[0] // copies, channels)
        sends = chunks.astype(jnp.bfloat16)
        mine = lax.dynamic_index_in_dim(chunks, rep, 0, keepdims=False)
        for far in range(1, copies):
            sent = lax.dynamic_index_in_dim(sends, rep ^ far, 0, keepdims=False)
            mine = mine + swap(sent, far, "rep").astype(jnp.float32)
        return mine

    mine = 0.0
    if last is not None:
        mine = swap(scattered(last).astype(jnp.bfloat16), 2 * (chips - 1)).astype(jnp.float32)
    mine = mine + scattered(sum(totals[1:], totals[0]))
    mine = mine.astype(jnp.bfloat16)
    gathered = [mine] + [swap(mine, far, "rep") for far in range(1, copies)]
    offset = 1
    while offset < copies:
        odd = (rep & offset) != 0
        gathered = [
            jnp.where(odd, gathered[at ^ offset], gathered[at]) for at in range(copies)
        ]
        offset *= 2
    summed = jnp.concatenate(gathered, axis=0).astype(jnp.float32)

    def turned(part):
        return jnp.swapaxes(part.reshape(9, channels, channels), 1, 2).reshape(1, taps, channels)

    tail = summed[2 * taps :]
    return (
        previous[0].reshape(acts.shape),
        previous[1].reshape(acts.shape),
        turned(summed[:taps]),
        turned(summed[taps : 2 * taps]),
        (tail[0] + tail[1])[None],
        (tail[2] + tail[3])[None],
    )


def solution(mesh):
    placed = (
        P(("rep", "member"), None, None, None),
        P(("rep", "member"), None, None, None),
        P(("rep", "member"), None),
        P("member", None, None),
        P("member", None, None),
        P("member", None),
        P("member", None),
    )
    return jax.shard_map(
        at_home if mesh.shape["member"] <= 8 else shards,
        mesh=mesh,
        in_specs=placed,
        out_specs=(
            P(("rep", "member"), None, None, None),
            P(("rep", "member"), None, None, None),
            P("member", None, None),
            P("member", None, None),
            P("member", None),
            P("member", None),
        ),
        check_vma=False,
    )
```

profile of v0, /device:TPU:0, one launch (start us, length us, event | category | flops | bytes accessed | tf_op | source)
XLA Modules:
  0.0 115.3 jit_solution(4677357460272173806)
XLA Ops:
  0.7 0.8 fusion.8
  1.4 0.1 concatenate.13
  1.6 2.0 %pad_maximum_fusion.weight_ref = bf16[2320,128]{1,0:T(8,128)(2,1)} fusion(bf16[16,128]{1,0:T(8,128)(2,1)S(1)} %concatenate.13, bf16[1152,128]{1,0:T(8,128)(2,1)} %bitcast.89, bf16[1152,128]{1,0:T(8,128)(2,1)} %bitcast.90), kind=kLoop, calls=%fused_computation.5 | loop fusion | flops 1781760 | bytes 1187840 | tf_op jit(solution)/shard_map/concatenate | solution.py:353
  3.6 0.5 collective-permute-start.6
  4.0 2.5 %collective-permute-start.4 = (bf16[2320,128]{1,0:T(8,128)(2,1)}, bf16[2320,128]{1,0:T(8,128)(2,1)}, u32[]{:S(2)}, u32[]{:S(2)}) collective-permute-start(bf16[2320,128]{1,0:T(8,128)(2,1)} %pad_maximum_fusion.weight_ref), channel_id=1, source_target_pairs={{0,2},{1,3},{2,0},{3,1},{4,6},{5,7},{6,4},{7,5},{8,10},{9,11},{10,... | collective-permute-start | bytes 1781768 | tf_op jit(solution)/shard_map/ppermute | solution.py:357
  6.5 1.5 %collective-permute-start.2 = (bf16[2320,128]{1,0:T(8,128)(2,1)}, bf16[2320,128]{1,0:T(8,128)(2,1)}, u32[]{:S(2)}, u32[]{:S(2)}) collective-permute-start(bf16[2320,128]{1,0:T(8,128)(2,1)} %pad_maximum_fusion.weight_ref), channel_id=1, source_target_pairs={{0,4},{1,5},{2,6},{3,7},{4,0},{5,1},{6,2},{7,3},{8,12},{9,13},{10,... | collective-permute-start | bytes 1781768 | tf_op jit(solution)/shard_map/ppermute | solution.py:357
  8.2 0.1 convert_reduce_fusion.1
  8.4 0.2 convert_reduce_fusion
  8.6 0.2 select_reduce_fusion
  8.9 0.1 copy.45
  9.0 0.1 copy.46
  9.3 4.8 %tower.8 = (bf16[32,100,128]{2,1,0:T(8,128)(2,1)S(1)}, bf16[32,100,128]{2,1,0:T(8,128)(2,1)S(1)}, bf16[2368,128]{1,0:T(8,128)(2,1)S(1)}) custom-call(s32[9]{0:T(128)S(1)} %get-tuple-element.86.slots_ref, bf16[32,100,128]{2,1,0:T(8,128)(2,1)S(1)} %bitcast.63, bf16[32,100,128]{2,1,0:T(8,128)(2,1)S(1)} %bitcast.71, bf16[2320,128]{1,0:T(8,128)(2,1)} %pad_maximum_fusion.weight_ref), custom_call_target="tpu_custom_call" | custom-call | flops 8493465600 | bytes 4000000 | tf_op jit(solution)/shard_map/tower/pallas_call | solution.py:296
  14.0 7.0 %collective-permute-done.4.weight_ref = bf16[2320,128]{1,0:T(8,128)(2,1)} collective-permute-done((bf16[2320,128]{1,0:T(8,128)(2,1)}, bf16[2320,128]{1,0:T(8,128)(2,1)}, u32[]{:S(2)}, u32[]{:S(2)}) %collective-permute-start.4) | collective-permute-done | bytes 593952 | tf_op jit(solution)/shard_map/ppermute | solution.py:357
  21.1 4.6 %tower.9 = (bf16[32,100,128]{2,1,0:T(8,128)(2,1)S(1)}, bf16[32,100,128]{2,1,0:T(8,128)(2,1)S(1)}, bf16[2368,128]{1,0:T(8,128)(2,1)S(1)}) custom-call(s32[9]{0:T(128)S(1)} %get-tuple-element.87.slots_ref, bf16[32,100,128]{2,1,0:T(8,128)(2,1)S(1)} %bitcast.64, bf16[32,100,128]{2,1,0:T(8,128)(2,1)S(1)} %bitcast.72, ...), custom_call_target="tpu_custom_call", output_to_operand_aliasing={{0}: (4, {}), {1}: (5, {})} | custom-call | flops 8493465600 | bytes 4000000 | tf_op jit(solution)/shard_map/tower/pallas_call | solution.py:296
  25.7 0.6 collective-permute-start.14
  26.3 8.8 %collective-permute-done.2.weight_ref = bf16[2320,128]{1,0:T(8,128)(2,1)} collective-permute-done((bf16[2320,128]{1,0:T(8,128)(2,1)}, bf16[2320,128]{1,0:T(8,128)(2,1)}, u32[]{:S(2)}, u32[]{:S(2)}) %collective-permute-start.2) | collective-permute-done | bytes 593952 | tf_op jit(solution)/shard_map/ppermute | solution.py:357
  35.1 0.5 collective-permute-start.1
  35.6 5.0 %tower.10 = (bf16[32,100,128]{2,1,0:T(8,128)(2,1)S(1)}, bf16[32,100,128]{2,1,0:T(8,128)(2,1)S(1)}, bf16[2368,128]{1,0:T(8,128)(2,1)S(1)}) custom-call(s32[9]{0:T(128)S(1)} %get-tuple-element.88.slots_ref, bf16[32,100,128]{2,1,0:T(8,128)(2,1)S(1)} %bitcast.65, bf16[32,100,128]{2,1,0:T(8,128)(2,1)S(1)} %bitcast.73, ...), custom_call_target="tpu_custom_call", output_to_operand_aliasing={{0}: (4, {}), {1}: (5, {})} | custom-call | flops 8493465600 | bytes 4000000 | tf_op jit(solution)/shard_map/tower/pallas_call | solution.py:296
  40.7 5.1 %tower.11 = (bf16[32,100,128]{2,1,0:T(8,128)(2,1)S(1)}, bf16[32,100,128]{2,1,0:T(8,128)(2,1)S(1)}, bf16[2368,128]{1,0:T(8,128)(2,1)S(1)}) custom-call(s32[9]{0:T(128)S(1)} %get-tuple-element.89.slots_ref, bf16[32,100,128]{2,1,0:T(8,128)(2,1)S(1)} %bitcast.66, bf16[32,100,128]{2,1,0:T(8,128)(2,1)S(1)} %bitcast.74, ...), custom_call_target="tpu_custom_call", output_to_operand_aliasing={{0}: (4, {}), {1}: (5, {})} | custom-call | flops 8493465600 | bytes 4000000 | tf_op jit(solution)/shard_map/tower/pallas_call | solution.py:296
  45.8 0.2 add_convert_fusion.1.rest_2_
  46.1 4.5 %tower.12 = (bf16[32,100,128]{2,1,0:T(8,128)(2,1)S(1)}, bf16[32,100,128]{2,1,0:T(8,128)(2,1)S(1)}, bf16[2368,128]{1,0:T(8,128)(2,1)S(1)}) custom-call(s32[9]{0:T(128)S(1)} %get-tuple-element.90.slots_ref, bf16[32,100,128]{2,1,0:T(8,128)(2,1)S(1)} %bitcast.67, bf16[32,100,128]{2,1,0:T(8,128)(2,1)S(1)} %bitcast.75, ...), custom_call_target="tpu_custom_call", output_to_operand_aliasing={{0}: (4, {}), {1}: (5, {})} | custom-call | flops 8493465600 | bytes 4000000 | tf_op jit(solution)/shard_map/tower/pallas_call | solution.py:296
  50.6 0.5 collective-permute-start.8
  51.1 4.6 %tower.13 = (bf16[32,100,128]{2,1,0:T(8,128)(2,1)S(1)}, bf16[32,100,128]{2,1,0:T(8,128)(2,1)S(1)}, bf16[2368,128]{1,0:T(8,128)(2,1)S(1)}) custom-call(s32[9]{0:T(128)S(1)} %get-tuple-element.91.slots_ref, bf16[32,100,128]{2,1,0:T(8,128)(2,1)S(1)} %bitcast.68, bf16[32,100,128]{2,1,0:T(8,128)(2,1)S(1)} %bitcast.76, ...), custom_call_target="tpu_custom_call", output_to_operand_aliasing={{0}: (4, {}), {1}: (5, {})} | custom-call | flops 8493465600 | bytes 4000000 | tf_op jit(solution)/shard_map/tower/pallas_call | solution.py:296
  55.7 0.2 add_convert_fusion.rest_2_
  55.9 0.8 collective-permute-start.16
  56.7 4.5 %tower.14 = (bf16[32,100,128]{2,1,0:T(8,128)(2,1)S(1)}, bf16[32,100,128]{2,1,0:T(8,128)(2,1)S(1)}, bf16[2368,128]{1,0:T(8,128)(2,1)S(1)}) custom-call(s32[9]{0:T(128)S(1)} %get-tuple-element.92.slots_ref, bf16[32,100,128]{2,1,0:T(8,128)(2,1)S(1)} %bitcast.69, bf16[32,100,128]{2,1,0:T(8,128)(2,1)S(1)} %bitcast.77, ...), custom_call_target="tpu_custom_call", output_to_operand_aliasing={{0}: (4, {}), {1}: (5, {})} | custom-call | flops 8493465600 | bytes 4000000 | tf_op jit(solution)/shard_map/tower/pallas_call | solution.py:296
  61.3 4.8 %tower.15 = (bf16[32,100,128]{2,1,0:T(8,128)(2,1)S(1)}, bf16[32,100,128]{2,1,0:T(8,128)(2,1)S(1)}, bf16[2368,128]{1,0:T(8,128)(2,1)S(1)}) custom-call(s32[9]{0:T(128)S(1)} %get-tuple-element.93.slots_ref, bf16[32,100,128]{2,1,0:T(8,128)(2,1)S(1)} %bitcast.70, bf16[32,100,128]{2,1,0:T(8,128)(2,1)S(1)} %bitcast.78, ...), custom_call_target="tpu_custom_call", output_to_operand_aliasing={{0}: (4, {}), {1}: (5, {})} | custom-call | flops 8493465600 | bytes 4000000 | tf_op jit(solution)/shard_map/tower/pallas_call | solution.py:296
  66.1 0.1 convert_add_fusion.1
  66.3 1.5 %collective-permute-start.10 = (bf16[592,128]{1,0:T(8,128)(2,1)S(1)}, bf16[592,128]{1,0:T(8,128)(2,1)S(1)}, u32[]{:S(2)}, u32[]{:S(2)}) collective-permute-start(bf16[592,128]{1,0:T(8,128)(2,1)S(1)} %get-tuple-element.80), channel_id=1, source_target_pairs={{0,8},{8,0},{16,24},{24,16},{1,9},{9,1},{17,25},{25,17},{2,10},{10... | collective-permute-start | bytes 454664 | tf_op jit(solution)/shard_map/ppermute | solution.py:357
  67.9 3.2 %collective-permute-start.11 = (bf16[592,128]{1,0:T(8,128)(2,1)S(1)}, bf16[592,128]{1,0:T(8,128)(2,1)S(1)}, u32[]{:S(2)}, u32[]{:S(2)}) collective-permute-start(bf16[592,128]{1,0:T(8,128)(2,1)S(1)} %get-tuple-element.82), channel_id=1, source_target_pairs={{0,16},{8,24},{16,0},{24,8},{1,17},{9,25},{17,1},{25,9},{2,18},{10... | collective-permute-start | bytes 454664 | tf_op jit(solution)/shard_map/ppermute | solution.py:357
  71.0 1.0 collective-permute-done.16
  72.0 0.3 convert_add_fusion
  72.4 1.7 %collective-permute-start.17 = (bf16[592,128]{1,0:T(8,128)(2,1)S(1)}, bf16[592,128]{1,0:T(8,128)(2,1)S(1)}, u32[]{:S(2)}, u32[]{:S(2)}) collective-permute-start(bf16[592,128]{1,0:T(8,128)(2,1)S(1)} %get-tuple-element.83), channel_id=1, source_target_pairs={{0,8},{8,0},{16,24},{24,16},{1,9},{9,1},{17,25},{25,17},{2,10},{10... | collective-permute-start | bytes 454664 | tf_op jit(solution)/shard_map/ppermute | solution.py:357
  74.1 2.7 %collective-permute-start.18 = (bf16[592,128]{1,0:T(8,128)(2,1)S(1)}, bf16[592,128]{1,0:T(8,128)(2,1)S(1)}, u32[]{:S(2)}, u32[]{:S(2)}) collective-permute-start(bf16[592,128]{1,0:T(8,128)(2,1)S(1)} %get-tuple-element.85), channel_id=1, source_target_pairs={{0,16},{8,24},{16,0},{24,8},{1,17},{9,25},{17,1},{25,9},{2,18},{10... | collective-permute-start | bytes 454664 | tf_op jit(solution)/shard_map/ppermute | solution.py:357
  76.8 1.8 %collective-permute-start.19 = (bf16[592,128]{1,0:T(8,128)(2,1)S(1)}, bf16[592,128]{1,0:T(8,128)(2,1)S(1)}, u32[]{:S(2)}, u32[]{:S(2)}) collective-permute-start(bf16[592,128]{1,0:T(8,128)(2,1)S(1)} %get-tuple-element.84), channel_id=1, source_target_pairs={{0,24},{8,16},{16,8},{24,0},{1,25},{9,17},{17,9},{25,1},{2,26},{10... | collective-permute-start | bytes 454664 | tf_op jit(solution)/shard_map/ppermute | solution.py:357
  78.6 3.7 %collective-permute-done.11 = bf16[592,128]{1,0:T(8,128)(2,1)S(1)} collective-permute-done((bf16[592,128]{1,0:T(8,128)(2,1)S(1)}, bf16[592,128]{1,0:T(8,128)(2,1)S(1)}, u32[]{:S(2)}, u32[]{:S(2)}) %collective-permute-start.11) | collective-permute-done | bytes 151584 | tf_op jit(solution)/shard_map/ppermute | solution.py:357
  82.4 2.7 %collective-permute-start.13 = (bf16[592,128]{1,0:T(8,128)(2,1)S(1)}, bf16[592,128]{1,0:T(8,128)(2,1)S(1)}, u32[]{:S(2)}, u32[]{:S(2)}) collective-permute-start(bf16[592,128]{1,0:T(8,128)(2,1)S(1)} %fusion.6), channel_id=1, source_target_pairs={{0,6},{1,7},{2,4},{3,5},{4,2},{5,3},{6,0},{7,1},{8,14},{9,15},{10,... | collective-permute-start | bytes 454664 | tf_op jit(solution)/shard_map/ppermute | solution.py:357
  85.1 10.2 %collective-permute-done.18 = bf16[592,128]{1,0:T(8,128)(2,1)S(1)} collective-permute-done((bf16[592,128]{1,0:T(8,128)(2,1)S(1)}, bf16[592,128]{1,0:T(8,128)(2,1)S(1)}, u32[]{:S(2)}, u32[]{:S(2)}) %collective-permute-start.18) | collective-permute-done | bytes 151584 | tf_op jit(solution)/shard_map/ppermute | solution.py:357
  95.3 0.1 fusion.3
  95.4 2.9 %collective-permute-start.20 = (bf16[592,128]{1,0:T(8,128)(2,1)S(1)}, bf16[592,128]{1,0:T(8,128)(2,1)S(1)}, u32[]{:S(2)}, u32[]{:S(2)}) collective-permute-start(bf16[592,128]{1,0:T(8,128)(2,1)S(1)} %fusion.3), channel_id=1, source_target_pairs={{0,24},{8,16},{16,8},{24,0},{1,25},{9,17},{17,9},{25,1},{2,26},{10... | collective-permute-start | bytes 454664 | tf_op jit(solution)/shard_map/ppermute | solution.py:357
  98.3 2.2 %collective-permute-start.21 = (bf16[592,128]{1,0:T(8,128)(2,1)S(1)}, bf16[592,128]{1,0:T(8,128)(2,1)S(1)}, u32[]{:S(2)}, u32[]{:S(2)}) collective-permute-start(bf16[592,128]{1,0:T(8,128)(2,1)S(1)} %fusion.3), channel_id=1, source_target_pairs={{0,16},{8,24},{16,0},{24,8},{1,17},{9,25},{17,1},{25,9},{2,18},{10... | collective-permute-start | bytes 454664 | tf_op jit(solution)/shard_map/ppermute | solution.py:357
  100.5 0.5 collective-permute-start.22
  101.0 1.5 %copy.49 = bf16[16,2,100,128]{3,1,2,0:T(2,128)(2,1)} copy(bf16[16,2,100,128]{3,2,1,0:T(8,128)(2,1)S(1)} %bitcast.79) | data formatting | bytes 1638400
  102.5 1.5 %copy.50 = bf16[16,2,100,128]{3,1,2,0:T(2,128)(2,1)} copy(bf16[16,2,100,128]{3,2,1,0:T(8,128)(2,1)S(1)} %bitcast.80) | data formatting | bytes 1638400
  104.0 8.4 %collective-permute-done.21 = bf16[592,128]{1,0:T(8,128)(2,1)S(1)} collective-permute-done((bf16[592,128]{1,0:T(8,128)(2,1)S(1)}, bf16[592,128]{1,0:T(8,128)(2,1)S(1)}, u32[]{:S(2)}, u32[]{:S(2)}) %collective-permute-start.21) | collective-permute-done | bytes 151584 | tf_op jit(solution)/shard_map/ppermute | solution.py:357
  112.5 0.5 convert_add_fusion.2
  113.2 1.1 copy.47
  114.2 1.0 copy.48
  (46 shorter events, 1.2 us)
Async XLA Ops:
  0.6 7.4 %copy-start.2 = (s32[16,2]{0,1:T(2,128)S(1)}, s32[16,2]{0,1:T(2,128)}, u32[]{:S(2)}) copy-start(s32[16,2]{0,1:T(2,128)} %param.9) | copy-start | bytes 388
  0.6 8.2 %copy-start = (bf16[16,2,100,128]{3,1,2,0:T(2,128)(2,1)S(1)}, bf16[16,2,100,128]{3,1,2,0:T(2,128)(2,1)}, u32[]{:S(2)}) copy-start(bf16[16,2,100,128]{3,1,2,0:T(2,128)(2,1)} %param.7) | copy-start | bytes 2457604
  1.6 7.4 %copy-start.1 = (bf16[16,2,100,128]{3,1,2,0:T(2,128)(2,1)S(1)}, bf16[16,2,100,128]{3,1,2,0:T(2,128)(2,1)}, u32[]{:S(2)}) copy-start(bf16[16,2,100,128]{3,1,2,0:T(2,128)(2,1)} %param.8) | copy-start | bytes 2457604
  3.6 17.5 %collective-permute-start.6 = (bf16[2320,128]{1,0:T(8,128)(2,1)}, bf16[2320,128]{1,0:T(8,128)(2,1)}, u32[]{:S(2)}, u32[]{:S(2)}) collective-permute-start(bf16[2320,128]{1,0:T(8,128)(2,1)} %pad_maximum_fusion.weight_ref), channel_id=1, source_target_pairs={{0,1},{1,0},{2,3},{3,2},{4,5},{5,4},{6,7},{7,6},{8,9},{9,8},{10,11... | collective-permute-start | bytes 1781768 | tf_op jit(solution)/shard_map/ppermute | solution.py:357
  4.0 17.1 %collective-permute-start.4 = (bf16[2320,128]{1,0:T(8,128)(2,1)}, bf16[2320,128]{1,0:T(8,128)(2,1)}, u32[]{:S(2)}, u32[]{:S(2)}) collective-permute-start(bf16[2320,128]{1,0:T(8,128)(2,1)} %pad_maximum_fusion.weight_ref), channel_id=1, source_target_pairs={{0,2},{1,3},{2,0},{3,1},{4,6},{5,7},{6,4},{7,5},{8,10},{9,11},{10,... | collective-permute-start | bytes 1781768 | tf_op jit(solution)/shard_map/ppermute | solution.py:357
  6.5 28.6 %collective-permute-start.2 = (bf16[2320,128]{1,0:T(8,128)(2,1)}, bf16[2320,128]{1,0:T(8,128)(2,1)}, u32[]{:S(2)}, u32[]{:S(2)}) collective-permute-start(bf16[2320,128]{1,0:T(8,128)(2,1)} %pad_maximum_fusion.weight_ref), channel_id=1, source_target_pairs={{0,4},{1,5},{2,6},{3,7},{4,0},{5,1},{6,2},{7,3},{8,12},{9,13},{10,... | collective-permute-start | bytes 1781768 | tf_op jit(solution)/shard_map/ppermute | solution.py:357
  8.0 27.1 %collective-permute-start = (bf16[2320,128]{1,0:T(8,128)(2,1)}, bf16[2320,128]{1,0:T(8,128)(2,1)}, u32[]{:S(2)}, u32[]{:S(2)}) collective-permute-start(bf16[2320,128]{1,0:T(8,128)(2,1)} %pad_maximum_fusion.weight_ref), channel_id=1, source_target_pairs={{0,6},{1,7},{2,4},{3,5},{4,2},{5,3},{6,0},{7,1},{8,14},{9,15},{10,... | collective-permute-start | bytes 1781768 | tf_op jit(solution)/shard_map/ppermute | solution.py:357
  21.1 14.5 %collective-permute-start.5 = (bf16[2320,128]{1,0:T(8,128)(2,1)}, bf16[2320,128]{1,0:T(8,128)(2,1)S(1)}, u32[]{:S(2)}, u32[]{:S(2)}) collective-permute-start(bf16[2320,128]{1,0:T(8,128)(2,1)} %collective-permute-done.4.weight_ref), channel_id=1, source_target_pairs={{0,1},{1,0},{2,3},{3,2},{4,5},{5,4},{6,7},{7,6},{8,9},{9,8},{10,11... | collective-permute-start | bytes 1781768 | tf_op jit(solution)/shard_map/ppermute | solution.py:357
  25.7 45.3 %collective-permute-start.14 = (bf16[2368,128]{1,0:T(8,128)(2,1)S(1)}, bf16[2368,128]{1,0:T(8,128)(2,1)S(1)}, u32[]{:S(2)}, u32[]{:S(2)}) collective-permute-start(bf16[2368,128]{1,0:T(8,128)(2,1)S(1)} %get-tuple-element.53), channel_id=1, source_target_pairs={{0,1},{1,0},{2,3},{3,2},{4,5},{5,4},{6,7},{7,6},{8,9},{9,8},{10,11... | collective-permute-start | bytes 1818632 | tf_op jit(solution)/shard_map/ppermute | solution.py:357
  35.1 11.0 %collective-permute-start.3 = (bf16[2320,128]{1,0:T(8,128)(2,1)}, bf16[2320,128]{1,0:T(8,128)(2,1)S(1)}, u32[]{:S(2)}, u32[]{:S(2)}) collective-permute-start(bf16[2320,128]{1,0:T(8,128)(2,1)} %collective-permute-done.2.weight_ref), channel_id=1, source_target_pairs={{0,1},{1,0},{2,3},{3,2},{4,5},{5,4},{6,7},{7,6},{8,9},{9,8},{10,11... | collective-permute-start | bytes 1781768 | tf_op jit(solution)/shard_map/ppermute | solution.py:357
  35.1 21.6 %collective-permute-start.1 = (bf16[2320,128]{1,0:T(8,128)(2,1)}, bf16[2320,128]{1,0:T(8,128)(2,1)S(1)}, u32[]{:S(2)}, u32[]{:S(2)}) collective-permute-start(bf16[2320,128]{1,0:T(8,128)(2,1)} %collective-permute-done.weight_ref), channel_id=1, source_target_pairs={{0,1},{1,0},{2,3},{3,2},{4,5},{5,4},{6,7},{7,6},{8,9},{9,8},{10,11... | collective-permute-start | bytes 1781768 | tf_op jit(solution)/shard_map/ppermute | solution.py:357
  40.6 5.2 %collective-permute-start.7 = (bf16[2368,128]{1,0:T(8,128)(2,1)S(1)}, bf16[2368,128]{1,0:T(8,128)(2,1)S(1)}, u32[]{:S(2)}, u32[]{:S(2)}) collective-permute-start(bf16[2368,128]{1,0:T(8,128)(2,1)S(1)} %get-tuple-element.39), channel_id=1, source_target_pairs={{0,1},{1,0},{2,3},{3,2},{4,5},{5,4},{6,7},{7,6},{8,9},{9,8},{10,11... | collective-permute-start | bytes 1818632 | tf_op jit(solution)/shard_map/ppermute | solution.py:357
  46.0 25.0 %collective-permute-start.15 = (bf16[2368,128]{1,0:T(8,128)(2,1)S(1)}, bf16[2368,128]{1,0:T(8,128)(2,1)S(1)}, u32[]{:S(2)}, u32[]{:S(2)}) collective-permute-start(bf16[2368,128]{1,0:T(8,128)(2,1)S(1)} %add_convert_fusion.1.rest_2_), channel_id=1, source_target_pairs={{0,2},{1,3},{2,0},{3,1},{4,6},{5,7},{6,4},{7,5},{8,10},{9,11},{10,... | collective-permute-start | bytes 1818632 | tf_op jit(solution)/shard_map/ppermute | solution.py:357
  50.6 5.1 %collective-permute-start.8 = (bf16[2368,128]{1,0:T(8,128)(2,1)S(1)}, bf16[2368,128]{1,0:T(8,128)(2,1)S(1)}, u32[]{:S(2)}, u32[]{:S(2)}) collective-permute-start(bf16[2368,128]{1,0:T(8,128)(2,1)S(1)} %get-tuple-element.45), channel_id=1, source_target_pairs={{0,1},{1,0},{2,3},{3,2},{4,5},{5,4},{6,7},{7,6},{8,9},{9,8},{10,11... | collective-permute-start | bytes 1818632 | tf_op jit(solution)/shard_map/ppermute | solution.py:357
  55.9 16.1 %collective-permute-start.16 = (bf16[2368,128]{1,0:T(8,128)(2,1)S(1)}, bf16[2368,128]{1,0:T(8,128)(2,1)S(1)}, u32[]{:S(2)}, u32[]{:S(2)}) collective-permute-start(bf16[2368,128]{1,0:T(8,128)(2,1)S(1)} %add_convert_fusion.rest_2_), channel_id=1, source_target_pairs={{0,4},{1,5},{2,6},{3,7},{4,0},{5,1},{6,2},{7,3},{8,12},{9,13},{10,... | collective-permute-start | bytes 1818632 | tf_op jit(solution)/shard_map/ppermute | solution.py:357
  61.2 4.9 %collective-permute-start.9 = (bf16[2368,128]{1,0:T(8,128)(2,1)S(1)}, bf16[2368,128]{1,0:T(8,128)(2,1)S(1)}, u32[]{:S(2)}, u32[]{:S(2)}) collective-permute-start(bf16[2368,128]{1,0:T(8,128)(2,1)S(1)} %get-tuple-element.51), channel_id=1, source_target_pairs={{0,1},{1,0},{2,3},{3,2},{4,5},{5,4},{6,7},{7,6},{8,9},{9,8},{10,11... | collective-permute-start | bytes 1818632 | tf_op jit(solution)/shard_map/ppermute | solution.py:357
  66.3 10.4 %collective-permute-start.10 = (bf16[592,128]{1,0:T(8,128)(2,1)S(1)}, bf16[592,128]{1,0:T(8,128)(2,1)S(1)}, u32[]{:S(2)}, u32[]{:S(2)}) collective-permute-start(bf16[592,128]{1,0:T(8,128)(2,1)S(1)} %get-tuple-element.80), channel_id=1, source_target_pairs={{0,8},{8,0},{16,24},{24,16},{1,9},{9,1},{17,25},{25,17},{2,10},{10... | collective-permute-start | bytes 454664 | tf_op jit(solution)/shard_map/ppermute | solution.py:357
  67.9 14.5 %collective-permute-start.11 = (bf16[592,128]{1,0:T(8,128)(2,1)S(1)}, bf16[592,128]{1,0:T(8,128)(2,1)S(1)}, u32[]{:S(2)}, u32[]{:S(2)}) collective-permute-start(bf16[592,128]{1,0:T(8,128)(2,1)S(1)} %get-tuple-element.82), channel_id=1, source_target_pairs={{0,16},{8,24},{16,0},{24,8},{1,17},{9,25},{17,1},{25,9},{2,18},{10... | collective-permute-start | bytes 454664 | tf_op jit(solution)/shard_map/ppermute | solution.py:357
  71.0 11.3 %collective-permute-start.12 = (bf16[592,128]{1,0:T(8,128)(2,1)S(1)}, bf16[592,128]{1,0:T(8,128)(2,1)S(1)}, u32[]{:S(2)}, u32[]{:S(2)}) collective-permute-start(bf16[592,128]{1,0:T(8,128)(2,1)S(1)} %get-tuple-element.81), channel_id=1, source_target_pairs={{0,24},{8,16},{16,8},{24,0},{1,25},{9,17},{17,9},{25,1},{2,26},{10... | collective-permute-start | bytes 454664 | tf_op jit(solution)/shard_map/ppermute | solution.py:357
  72.4 12.6 %collective-permute-start.17 = (bf16[592,128]{1,0:T(8,128)(2,1)S(1)}, bf16[592,128]{1,0:T(8,128)(2,1)S(1)}, u32[]{:S(2)}, u32[]{:S(2)}) collective-permute-start(bf16[592,128]{1,0:T(8,128)(2,1)S(1)} %get-tuple-element.83), channel_id=1, source_target_pairs={{0,8},{8,0},{16,24},{24,16},{1,9},{9,1},{17,25},{25,17},{2,10},{10... | collective-permute-start | bytes 454664 | tf_op jit(solution)/shard_map/ppermute | solution.py:357
  74.1 21.2 %collective-permute-start.18 = (bf16[592,128]{1,0:T(8,128)(2,1)S(1)}, bf16[592,128]{1,0:T(8,128)(2,1)S(1)}, u32[]{:S(2)}, u32[]{:S(2)}) collective-permute-start(bf16[592,128]{1,0:T(8,128)(2,1)S(1)} %get-tuple-element.85), channel_id=1, source_target_pairs={{0,16},{8,24},{16,0},{24,8},{1,17},{9,25},{17,1},{25,9},{2,18},{10... | collective-permute-start | bytes 454664 | tf_op jit(solution)/shard_map/ppermute | solution.py:357
  76.8 18.5 %collective-permute-start.19 = (bf16[592,128]{1,0:T(8,128)(2,1)S(1)}, bf16[592,128]{1,0:T(8,128)(2,1)S(1)}, u32[]{:S(2)}, u32[]{:S(2)}) collective-permute-start(bf16[592,128]{1,0:T(8,128)(2,1)S(1)} %get-tuple-element.84), channel_id=1, source_target_pairs={{0,24},{8,16},{16,8},{24,0},{1,25},{9,17},{17,9},{25,1},{2,26},{10... | collective-permute-start | bytes 454664 | tf_op jit(solution)/shard_map/ppermute | solution.py:357
  82.4 12.9 %collective-permute-start.13 = (bf16[592,128]{1,0:T(8,128)(2,1)S(1)}, bf16[592,128]{1,0:T(8,128)(2,1)S(1)}, u32[]{:S(2)}, u32[]{:S(2)}) collective-permute-start(bf16[592,128]{1,0:T(8,128)(2,1)S(1)} %fusion.6), channel_id=1, source_target_pairs={{0,6},{1,7},{2,4},{3,5},{4,2},{5,3},{6,0},{7,1},{8,14},{9,15},{10,... | collective-permute-start | bytes 454664 | tf_op jit(solution)/shard_map/ppermute | solution.py:357
  95.4 8.6 %collective-permute-start.20 = (bf16[592,128]{1,0:T(8,128)(2,1)S(1)}, bf16[592,128]{1,0:T(8,128)(2,1)S(1)}, u32[]{:S(2)}, u32[]{:S(2)}) collective-permute-start(bf16[592,128]{1,0:T(8,128)(2,1)S(1)} %fusion.3), channel_id=1, source_target_pairs={{0,24},{8,16},{16,8},{24,0},{1,25},{9,17},{17,9},{25,1},{2,26},{10... | collective-permute-start | bytes 454664 | tf_op jit(solution)/shard_map/ppermute | solution.py:357
  98.3 14.1 %collective-permute-start.21 = (bf16[592,128]{1,0:T(8,128)(2,1)S(1)}, bf16[592,128]{1,0:T(8,128)(2,1)S(1)}, u32[]{:S(2)}, u32[]{:S(2)}) collective-permute-start(bf16[592,128]{1,0:T(8,128)(2,1)S(1)} %fusion.3), channel_id=1, source_target_pairs={{0,16},{8,24},{16,0},{24,8},{1,17},{9,25},{17,1},{25,9},{2,18},{10... | collective-permute-start | bytes 454664 | tf_op jit(solution)/shard_map/ppermute | solution.py:357
  100.5 11.9 %collective-permute-start.22 = (bf16[592,128]{1,0:T(8,128)(2,1)S(1)}, bf16[592,128]{1,0:T(8,128)(2,1)S(1)}, u32[]{:S(2)}, u32[]{:S(2)}) collective-permute-start(bf16[592,128]{1,0:T(8,128)(2,1)S(1)} %fusion.3), channel_id=1, source_target_pairs={{0,8},{8,0},{16,24},{24,16},{1,9},{9,1},{17,25},{25,17},{2,10},{10... | collective-permute-start | bytes 454664 | tf_op jit(solution)/shard_map/ppermute | solution.py:357
where the time goes:
time: 115 us
  waiting for transfers between devices  39.2 us (34%)
  Pallas kernels  37.9 us (33%)
  starting transfers between devices  26.2 us (23%)
  local copies, waits for them, and re-layouts  5.98 us (5%)
  other arithmetic  5.1 us (4%)
    ppermute x23, waiting for transfers between devices, swap(): return lax.ppermute(value, axis, [(i, i ^ offset) for i in range(size)])  39.2 us
    pallas_call x8, Pallas kernels, tower(): pl.pallas_call(functools.partial(tower_kernel, extra), out_shape=(rows_sh...  37.9 us
    ppermute x23, starting transfers between devices, swap(): return lax.ppermute(value, axis, [(i, i ^ offset) for i in range(size)])  26.2 us
    unnamed x11, local copies, waits for them, and re-layouts  3.37 us
  transfers between devices with their start and end apart: 23, of which 6 were waited for; matrix products, arithmetic and copies ran while one was open for 5% of the time, Pallas kernels for 33%

commit v1 on v0

v1 whole, which is shorter than its diff:
```python
import functools

import jax
import jax.numpy as jnp
from jax import lax
from jax.experimental import pallas as pl
from jax.experimental.pallas import tpu as pltpu
from jax.sharding import PartitionSpec as P

BOARD = 10


def flipped(weight):
    channels = weight.shape[-1]
    stacked = weight.reshape(weight.shape[:-2] + (9, channels, channels))
    reversed_taps = jnp.flip(stacked, axis=-3)
    return jnp.swapaxes(reversed_taps, -1, -2).reshape(weight.shape)


def silu_slope(pre_act):
    sigmoid_vals = jax.nn.sigmoid(pre_act)
    return sigmoid_vals * (1.0 + pre_act * (1.0 - sigmoid_vals))


def board_conv(values, weight):
    count = values.shape[0]
    channels = values.shape[-1]
    side = BOARD
    boards = values.reshape(count, side, side, channels)
    kernel = weight.reshape(3, 3, channels, channels)
    result = lax.conv_general_dilated(
        boards,
        kernel,
        (1, 1),
        ((1, 1), (1, 1)),
        dimension_numbers=("NHWC", "HWIO", "NHWC"),
        preferred_element_type=jnp.float32,
    )
    return result.reshape(count, side * side, channels)


def weight_conv(values, grads):
    count = values.shape[0]
    channels = values.shape[-1]
    side = BOARD
    boards = values.reshape(count, side, side, channels)
    grad_boards = grads.reshape(count, side, side, channels)
    result = lax.conv_general_dilated(
        boards,
        grad_boards,
        (1, 1),
        ((1, 1), (1, 1)),
        dimension_numbers=("CHWN", "IHWO", "NHWC"),
        preferred_element_type=jnp.float32,
    )
    return jnp.transpose(result, (1, 2, 0, 3)).reshape(9 * channels, channels)


def shards(acts, cotangent, routes, w_first, w_second, b_first, b_second):
    per_owner = w_first.shape[0]
    owners = lax.axis_size("member")
    members_all = owners * per_owner
    capacity = max(2, 4 * routes.shape[0] // members_all)
    channels = acts.shape[-1]
    cell_count = acts.shape[-2]
    member_ids = routes.reshape(-1)
    onehot = (member_ids[:, None] == jnp.arange(members_all, dtype=jnp.int32)[None, :]).astype(
        jnp.int32
    )
    order = jnp.arange(member_ids.shape[0], dtype=jnp.int32)
    earlier = jnp.sum((order[:, None] > order[None, :])[:, :, None] * onehot[None], axis=1)
    slot_index = jnp.sum(earlier * onehot, axis=1)
    target = member_ids * capacity + slot_index
    dispatch = (
        jnp.arange(members_all * capacity, dtype=jnp.int32)[:, None] == target[None, :]
    ).astype(jnp.bfloat16)

    def scatter_rows(values):
        flattened = values.reshape(-1, cell_count * channels)
        placed = jnp.dot(dispatch, flattened, preferred_element_type=jnp.float32).astype(
            jnp.bfloat16
        )
        return placed.reshape(members_all, capacity, cell_count, channels)

    def gather_rows(values):
        flattened = values.reshape(members_all * capacity, cell_count * channels)
        picked = jnp.dot(dispatch.T, flattened, preferred_element_type=jnp.float32).astype(
            jnp.bfloat16
        )
        return picked.reshape(acts.shape)

    def to_local(received):
        grouped = received.reshape(owners, per_owner, capacity, cell_count, channels)
        return jnp.swapaxes(grouped, 0, 1).reshape(
            per_owner, owners * capacity, cell_count, channels
        )

    def from_local(values):
        grouped = values.reshape(per_owner, owners, capacity, cell_count, channels)
        return jnp.swapaxes(grouped, 0, 1).reshape(members_all, capacity, cell_count, channels)

    send_acts = scatter_rows(acts)
    send_grads = scatter_rows(cotangent)
    recv_acts, recv_grads = (
        lax.all_to_all(send_acts, "member", split_axis=0, concat_axis=0, tiled=True),
        lax.all_to_all(send_grads, "member", split_axis=0, concat_axis=0, tiled=True),
    )
    inputs = to_local(recv_acts)
    upstream = to_local(recv_grads)
    owned = 0
    pre_one = board_conv(inputs[owned], w_first[owned]) + b_first[owned][None, None, :]
    hidden_one = jax.nn.silu(pre_one).astype(jnp.bfloat16)
    result_one = (
        inputs[owned].astype(jnp.float32)
        + board_conv(hidden_one, w_second[owned])
        + b_second[owned][None, None, :]
    ).astype(jnp.bfloat16)
    pre_list = [pre_one]
    hidden_list = [hidden_one]
    result_list = [result_one]
    result = jnp.stack(result_list)
    owned = 0
    upstream_one = upstream[owned]
    grad_two_list = [weight_conv(hidden_list[owned], upstream_one)]
    bias_two_list = [jnp.sum(upstream_one.astype(jnp.float32), axis=(0, 1))]
    hidden_grad = board_conv(upstream_one, flipped(w_second[owned]))
    pre_grad = (hidden_grad * silu_slope(pre_list[owned])).astype(jnp.bfloat16)
    grad_one_list = [weight_conv(inputs[owned], pre_grad)]
    bias_one_list = [jnp.sum(pre_grad.astype(jnp.float32), axis=(0, 1))]
    input_list = [
        (upstream_one.astype(jnp.float32) + board_conv(pre_grad, flipped(w_first[owned]))).astype(
            jnp.bfloat16
        )
    ]
    input_grad = jnp.stack(input_list)
    grad_one = jnp.stack(grad_one_list)
    grad_two = jnp.stack(grad_two_list)
    bias_one = jnp.stack(bias_one_list)
    bias_two = jnp.stack(bias_two_list)
    back_out, back_in = (
        lax.all_to_all(from_local(result), "member", split_axis=0, concat_axis=0, tiled=True),
        lax.all_to_all(from_local(input_grad), "member", split_axis=0, concat_axis=0, tiled=True),
    )
    totals = lax.psum((grad_one, grad_two, bias_one, bias_two), "rep")
    return (gather_rows(back_out), gather_rows(back_in), totals[0], totals[1], totals[2], totals[3])


SLOTS = 8
SIDE = BOARD + 2
CELLS = BOARD * BOARD
ROWS = CELLS * SLOTS
LINE = BOARD * SLOTS
PLACES = SIDE * SIDE * SLOTS
TAIL = 64
MESH_ID = pl.DeviceIdType.MESH

ORDER = (
    ["A0", "A1", "B0", "C0", "A2", "A4", "A3", "A5", "A6", "A7"]
    + ["B2", "B4", "C2", "B6", "B7", "B3", "B5", "B1"]
    + ["C1", "C4", "C3", "C5", "C6", "C7"]
)
AT = {name: index for index, name in enumerate(ORDER)}


def inner(line):
    return ((line + 1) * SIDE + 1) * SLOTS


def wide(lhs, rhs):
    return lax.dot_general(lhs, rhs, (((1,), (1,)), ((), ())), preferred_element_type=jnp.float32)


def league_kernel(
    table, acts_in, cot_in, w1_in, w2_in, b_in,
    out_ref, back_ref, grad_one, grad_two, bias_one, bias_two,
    acts, cot, w1, w2, bs, xb, gb, hb, pb, slope, mix, res_out, res_back,
    even, odd, paired, chips, diag, cross, total, split, parts, whole,
    load_sems, w_send, w_recv, g_send, g_recv, z_send, z_recv,
):
    f32, bf16 = jnp.float32, jnp.bfloat16
    channels = w1.shape[-1]
    taps = 9 * channels
    half_w = taps // 2
    rows_g = taps + TAIL
    half_g = rows_g // 2
    copies = whole.shape[1]
    quarter = rows_g // copies
    me = lax.axis_index("member")
    rep = lax.axis_index("rep")
    near = {"core": me ^ 1, "x": me ^ 2, "y": me ^ 4}

    loads = [
        pltpu.make_async_copy(src, dst, load_sems.at[at])
        for at, (src, dst) in enumerate(
            ((acts_in, acts), (cot_in, cot), (w1_in.at[0], w1.at[0]), (w2_in.at[0], w2.at[0]), (b_in, bs.at[0]))
        )
    ]
    for load in loads:
        load.start()

    barrier = pltpu.get_barrier_semaphore()
    for peer in near.values():
        pl.semaphore_signal(barrier, inc=1, device_id={"member": peer}, device_id_type=MESH_ID)
    for far in range(1, copies):
        pl.semaphore_signal(barrier, inc=1, device_id={"rep": rep ^ far}, device_id_type=MESH_ID)

    for ref in (xb, gb, hb, pb):
        ref[...] = jnp.zeros_like(ref)
    for load in loads:
        load.wait()
    pl.semaphore_wait(barrier, 2 + copies)

    def remote(src, dst, sends, recvs, at, peer):
        return pltpu.make_async_remote_copy(
            src_ref=src, dst_ref=dst, send_sem=sends.at[at], recv_sem=recvs.at[at],
            device_id=peer, device_id_type=MESH_ID,
        )

    def member(name):
        return {"member": near[name]}

    low, high = pl.ds(0, half_w), pl.ds(half_w, taps - half_w)

    def give(kind, at):
        buffer = (w1, w2, bs)[kind]
        moves = [
            (0, 1, None, "core"), (0, 2, None, "x"), (0, 4, None, "y"),
            (2, 3, None, "core"), (4, 5, None, "core"),
            (2, 6, low, "y"), (4, 6, high, "x"), (6, 7, None, "core"),
        ]
        src, dst, rows, peer = moves[at]
        if kind == 2 or rows is None:
            pair = (buffer.at[src], buffer.at[dst])
        else:
            pair = (buffer.at[src, rows, :], buffer.at[dst, rows, :])
        return remote(pair[0], pair[1], w_send, w_recv, kind * 8 + at, member(peer))

    def biases(ats):
        return [at for at in ats if at != 6]

    def send_weights(kind, ats):
        for at in ats:
            give(kind, at).start()
        if kind == 0:
            for at in biases(ats):
                give(2, at).start()

    def have_weights(kind, ats):
        for at in ats:
            give(kind, at).wait_recv()
        if kind == 0:
            for at in biases(ats):
                give(2, at).wait_recv()

    first, second = pl.ds(0, half_g), pl.ds(half_g, half_g)

    def grad_copy(j, at):
        if at < 4:
            return remote(odd.at[j, at], paired.at[j, at], g_send, g_recv, j * 8 + at, member("core"))
        if at == 4:
            return remote(chips.at[j, 3, first, :], diag.at[j, 0], g_send, g_recv, j * 8 + 4, member("x"))
        if at == 5:
            return remote(chips.at[j, 3, second, :], diag.at[j, 1], g_send, g_recv, j * 8 + 5, member("y"))
        return remote(
            chips.at[j, at - 5], cross.at[j, at - 6], g_send, g_recv, j * 8 + at, member("x" if at == 6 else "y")
        )

    def rep_copy(j, stage, far):
        at = (j * 2 + stage) * copies + far
        peer = {"rep": rep ^ far}
        if stage == 0:
            return remote(
                split.at[j, pl.ds((rep ^ far) * quarter, quarter), :], parts.at[j, far - 1], z_send, z_recv, at, peer
            )
        return remote(whole.at[j, rep], whole.at[j, rep], z_send, z_recv, at, peer)

    def arrived_rep(j, far):
        return remote(
            whole.at[j, rep], whole.at[j, rep ^ far], z_send, z_recv, (j * 2 + 1) * copies + far, {"rep": rep ^ far}
        )

    def pair_up(j, p):
        grad_copy(j, p).wait_recv()
        return even[j, p] + paired[j, p].astype(f32)

    def send_diag(j):
        chips[j, 3] = pair_up(j, 3).astype(bf16)
        grad_copy(j, 4).start()
        grad_copy(j, 5).start()

    def send_cross(j, p):
        value = pair_up(j, p)
        if p == 1:
            grad_copy(j, 5).wait_recv()
            chips[j, 1, :half_g] = value[:half_g].astype(bf16)
            chips[j, 1, half_g:] = (value[half_g:] + diag[j, 1].astype(f32)).astype(bf16)
            grad_copy(j, 6).start()
        else:
            grad_copy(j, 4).wait_recv()
            chips[j, 2, :half_g] = (value[:half_g] + diag[j, 0].astype(f32)).astype(bf16)
            chips[j, 2, half_g:] = value[half_g:].astype(bf16)
            grad_copy(j, 7).start()

    def send_split(j):
        value = pair_up(j, 0)
        grad_copy(j, 6).wait_recv()
        grad_copy(j, 7).wait_recv()
        value = value + cross[j, 0].astype(f32) + cross[j, 1].astype(f32)
        total[j] = value
        split[j] = value.astype(bf16)
        for far in range(1, copies):
            rep_copy(j, 0, far).start()

    def send_whole(j):
        mine = total[j, pl.ds(rep * quarter, quarter), :]
        for far in range(1, copies):
            rep_copy(j, 0, far).wait_recv()
            mine = mine + parts[j, far - 1].astype(f32)
        whole[j, rep] = mine.astype(bf16)
        for far in range(1, copies):
            rep_copy(j, 1, far).start()

    def finish(j):
        grad, bias = ((grad_one, bias_one), (grad_two, bias_two))[j]
        for far in range(1, copies):
            arrived_rep(j, far).wait_recv()
        stacked = jnp.concatenate([whole[j, at] for at in range(copies)], axis=0).astype(f32)
        for tap in range(9):
            rows = slice(tap * channels, (tap + 1) * channels)
            grad[0, rows, :] = stacked[rows].T
        bias[...] = whole[j, copies - 1, quarter - TAIL : quarter - TAIL + 8].astype(f32)[:1]

    def patch(board, q):
        columns = []
        for tap in range(9):
            down, right = tap // 3, tap % 3
            lines = []
            for line in range(BOARD):
                start = ((line + down) * SIDE + right) * SLOTS
                lines.append(board[q, start : start + LINE, :])
            columns.append(jnp.concatenate(lines, axis=0))
        return jnp.concatenate(columns, axis=1)

    def put(board, q, value):
        for line in range(BOARD):
            board[q, inner(line) : inner(line) + LINE, :] = value[line * LINE : (line + 1) * LINE].astype(bf16)

    def centre(board, q):
        return jnp.concatenate(
            [board[q, inner(line) : inner(line) + LINE, :] for line in range(BOARD)], axis=0
        ).astype(f32)

    def flipped_wide(weight, q):
        return jnp.concatenate(
            [weight[q, (8 - tap) * channels : (9 - tap) * channels, :] for tap in range(9)], axis=1
        )

    def gather(src, board, q):
        for slot in range(SLOTS):
            row = table[q * SLOTS + slot]
            value = src[jnp.maximum(row, 0)].astype(f32)
            mix[pl.ds(slot, CELLS, stride=SLOTS), :] = jnp.where(row >= 0, value, 0.0)
        put(board, q, mix[...])

    def spread(ref, q, value):
        mix[...] = value
        for slot in range(SLOTS):
            ref[q * SLOTS + slot] = mix[pl.ds(slot, CELLS, stride=SLOTS), :].astype(bf16)

    def keep_grad(j, q, grad, patches):
        turned = jnp.dot(grad.T.astype(bf16), patches, preferred_element_type=f32)
        bias = jnp.broadcast_to(jnp.sum(grad, axis=0, keepdims=True), (TAIL, channels))
        pair = q // 2

        def write(ref, kind):
            for tap in range(9):
                ref[j, pair, tap * channels : (tap + 1) * channels, :] = turned[
                    :, tap * channels : (tap + 1) * channels
                ].astype(kind)
            ref[j, pair, taps:, :] = bias.astype(kind)

        @pl.when(q % 2 == 0)
        def _():
            write(even, f32)

        @pl.when(q % 2 == 1)
        def _():
            write(odd, bf16)

    def phase_a(q):
        gather(acts, xb, q)
        gather(cot, gb, q)
        pre = jnp.dot(patch(xb, q), w1[q], preferred_element_type=f32) + bs[q, 0:1]
        gate = 0.5 * jnp.tanh(0.5 * pre) + 0.5
        slope[q] = gate * (1.0 + pre * (1.0 - gate))
        put(hb, q, pre * gate)
        keep_grad(1, q, centre(gb, q), patch(hb, q))

    def phase_b(q):
        pre_grad = wide(patch(gb, q), flipped_wide(w2, q)) * slope[q]
        put(pb, q, pre_grad)
        keep_grad(0, q, pre_grad.astype(bf16).astype(f32), patch(xb, q))

    def phase_c(q):
        spread(
            res_out, q,
            jnp.dot(patch(hb, q), w2[q], preferred_element_type=f32) + bs[q, 1:2] + centre(xb, q),
        )
        spread(res_back, q, wide(patch(pb, q), flipped_wide(w1, q)) + centre(gb, q))

    before = {name: [] for name in ORDER}

    def on(name, action, *args):
        before[name].append(functools.partial(action, *args))

    send_weights(0, (1, 2, 0))
    on("A1", have_weights, 0, (0,))
    on("A2", have_weights, 0, (1, 2))
    on("A2", send_weights, 0, (5, 6, 3, 4))
    on("A2", send_weights, 1, (1, 2, 0))
    on("A3", have_weights, 0, (3,))
    on("A5", have_weights, 0, (4,))
    on("A6", have_weights, 0, (5, 6))
    on("A6", send_weights, 0, (7,))
    on("A7", have_weights, 0, (7,))
    on("B2", have_weights, 1, (1, 2))
    on("B2", send_weights, 1, (5, 6, 3, 4))
    on("B6", have_weights, 1, (5, 6))
    on("B6", send_weights, 1, (7,))
    on("B7", have_weights, 1, (7,))
    on("B3", have_weights, 1, (3,))
    on("B5", have_weights, 1, (4,))
    on("B1", have_weights, 1, (0,))

    for j, phase in ((1, "A"), (0, "B")):
        for p in range(4):
            done = AT[phase + str(2 * p + 1)]
            on(ORDER[done + 1], lambda j=j, p=p: grad_copy(j, p).start())

    on("B4", send_diag, 1)
    on("B6", send_cross, 1, 1)
    on("B6", send_cross, 1, 2)
    on("B5", send_diag, 0)
    on("C1", send_split, 1)
    on("C1", send_cross, 0, 1)
    on("C4", send_cross, 0, 2)
    on("C5", send_whole, 1)
    on("C7", send_split, 0)

    phases = {"A": phase_a, "B": phase_b, "C": phase_c}

    def step(at, carry):
        q = jnp.int32(0)
        kind = jnp.int32(0)
        for index, name in enumerate(ORDER):
            q = jnp.where(at == index, int(name[1]), q)
            kind = jnp.where(at == index, "ABC".index(name[0]), kind)
            if before[name]:

                @pl.when(at == index)
                def _(name=name):
                    for action in before[name]:
                        action()

        for index, name in enumerate("ABC"):

            @pl.when(kind == index)
            def _(name=name):
                phases[name](q)

        return carry

    lax.fori_loop(0, len(ORDER), step, 0)

    send_whole(0)
    for row in range(out_ref.shape[0]):
        at = table[8 * SLOTS + row]
        out_ref[row] = res_out[at]
        back_ref[row] = res_back[at]
    finish(1)
    finish(0)

    for kind in range(3):
        for at in range(8):
            if kind < 2 or at != 6:
                give(kind, at).wait_send()
    for j in range(2):
        for at in range(8):
            grad_copy(j, at).wait_send()
        for stage in range(2):
            for far in range(1, copies):
                rep_copy(j, stage, far).wait_send()


def at_home(acts, cotangent, routes, w_first, w_second, b_first, b_second):
    owners = lax.axis_size("member")
    copies = lax.axis_size("rep")
    channels = acts.shape[-1]
    taps = 9 * channels
    rows_g = taps + TAIL
    f32, bf16 = jnp.float32, jnp.bfloat16
    me = lax.axis_index("member")
    ids = routes.reshape(-1)
    count = ids.shape[0]
    order = jnp.arange(count, dtype=jnp.int32)
    place = jnp.sum(((order[:, None] > order[None, :]) & (ids[:, None] == ids[None, :])).astype(jnp.int32), axis=1)
    position = (ids ^ me) * SLOTS + place
    hit = position[None, :] == jnp.arange(owners * SLOTS, dtype=jnp.int32)[:, None]
    rows = jnp.sum(jnp.where(hit, order[None, :] + 1, 0), axis=1) - 1
    table = jnp.concatenate([rows, position])
    biases = jnp.concatenate([b_first, b_second, jnp.zeros((6, channels), f32)], axis=0)

    x = acts.reshape((count,) + acts.shape[2:])
    g = cotangent.reshape((count,) + acts.shape[2:])
    anywhere = pl.BlockSpec(memory_space=pl.ANY)
    vmem = pl.BlockSpec(memory_space=pltpu.VMEM)
    shape = jax.ShapeDtypeStruct
    board = pltpu.VMEM((owners, PLACES, channels), bf16)
    weight = pltpu.VMEM((owners, taps, channels), bf16)
    results = pltpu.VMEM((owners * SLOTS, CELLS, channels), bf16)
    sems = pltpu.SemaphoreType.DMA
    made = pl.pallas_call(
        league_kernel,
        out_shape=(
            shape(x.shape, bf16),
            shape(x.shape, bf16),
            shape((1, taps, channels), f32),
            shape((1, taps, channels), f32),
            shape((1, channels), f32),
            shape((1, channels), f32),
        ),
        in_specs=[pl.BlockSpec(memory_space=pltpu.SMEM)] + [anywhere] * 5,
        out_specs=(vmem,) * 6,
        scratch_shapes=[
            pltpu.VMEM(x.shape, bf16),
            pltpu.VMEM(x.shape, bf16),
            weight,
            weight,
            pltpu.VMEM((owners, 8, channels), f32),
            board,
            board,
            board,
            board,
            pltpu.VMEM((owners, ROWS, channels), f32),
            pltpu.VMEM((ROWS, channels), f32),
            results,
            results,
            pltpu.VMEM((2, 4, rows_g, channels), f32),
            pltpu.VMEM((2, 4, rows_g, channels), bf16),
            pltpu.VMEM((2, 4, rows_g, channels), bf16),
            pltpu.VMEM((2, 4, rows_g, channels), bf16),
            pltpu.VMEM((2, 2, rows_g // 2, channels), bf16),
            pltpu.VMEM((2, 2, rows_g, channels), bf16),
            pltpu.VMEM((2, rows_g, channels), f32),
            pltpu.VMEM((2, rows_g, channels), bf16),
            pltpu.VMEM((2, copies - 1, rows_g // copies, channels), bf16),
            pltpu.VMEM((2, copies, rows_g // copies, channels), bf16),
            sems((5,)),
            sems((24,)),
            sems((24,)),
            sems((16,)),
            sems((16,)),
            sems((4 * copies,)),
            sems((4 * copies,)),
        ],
        compiler_params=pltpu.CompilerParams(
            collective_id=0, has_side_effects=True, vmem_limit_bytes=60 * 1024 * 1024
        ),
        cost_estimate=pl.CostEstimate(
            flops=12 * owners * ROWS * taps * channels, bytes_accessed=9000000, transcendentals=owners * ROWS * channels
        ),
        name="league",
    )(table, x, g, w_first, w_second, biases)
    return (made[0].reshape(acts.shape), made[1].reshape(acts.shape)) + tuple(made[2:])


def solution(mesh):
    placed = (
        P(("rep", "member"), None, None, None),
        P(("rep", "member"), None, None, None),
        P(("rep", "member"), None),
        P("member", None, None),
        P("member", None, None),
        P("member", None),
        P("member", None),
    )
    return jax.shard_map(
        at_home if mesh.shape["member"] == 8 and mesh.shape["rep"] == 4 else shards,
        mesh=mesh,
        in_specs=placed,
        out_specs=(
            P(("rep", "member"), None, None, None),
            P(("rep", "member"), None, None, None),
            P("member", None, None),
            P("member", None, None),
            P("member", None),
            P("member", None),
        ),
        check_vma=False,
    )
```

time: 115 us -> 91.1 us (0.79)
  Pallas kernels: 37.9 us -> 77.5 us
  waiting for transfers between devices: 39.2 us -> 0 us
  starting transfers between devices: 26.2 us -> 0 us
  local copies, waits for them, and re-layouts: 5.98 us -> 11.6 us
  other arithmetic: 5.1 us -> 1.53 us
    pallas_call x8 -> x1, Pallas kernels: 37.9 us -> 77.5 us  [at_home(): pl.pallas_call(league_kernel, out_shape=(shape(x.shape, bf16), shape(x.sh...]
    ppermute x23 -> x0, waiting for transfers between devices: 39.2 us -> none  [swap(): return lax.ppermute(value, axis, [(i, i ^ offset) for i in range(size)])]
    ppermute x23 -> x0, starting transfers between devices: 26.2 us -> none  [swap(): return lax.ppermute(value, axis, [(i, i ^ offset) for i in range(size)])]
    unnamed x11 -> x27, local copies, waits for them, and re-layouts: 3.37 us -> 11.5 us
    transpose x2 -> x0, local copies, waits for them, and re-layouts: 2.1 us -> none  [turned(): jnp.swapaxes(part.reshape(9, channels, channels), 1, 2)]
    convert_element_type x8 -> x0, other arithmetic: 1.49 us -> none  [the longest x1 0.76 us: at_home(): piece.astype(jnp.bfloat16)]
  transfers between devices with their start and end apart: 23 -> 0, of which waited for: 6 -> 0; matrix products, arithmetic and copies ran while one was open for 5% -> 0% of each run, Pallas kernels for 33% -> 0%
where the time goes in v1:
time: 91.1 us; the launch traced here: 91.3 us
  Pallas kernels  77.5 us (85%)
  local copies, waits for them, and re-layouts  11.6 us (13%)
  other arithmetic  1.53 us (2%)
    pallas_call x1, Pallas kernels, at_home(): pl.pallas_call(league_kernel, out_shape=(shape(x.shape, bf16), shape(x.sh...  77.5 us
    unnamed x27, local copies, waits for them, and re-layouts  11.5 us

profile of v1, /device:TPU:0, one launch (start us, length us, event | category | flops | bytes accessed | tf_op | source)
XLA Modules:
  0.0 91.3 jit_solution(285682853786055568)
XLA Ops:
  0.6 0.0 copy-start.5
  0.7 0.0 copy-start.6
  0.7 0.1 pad.2.clone
  0.7 0.6 copy-done.5
  1.3 0.0 copy-done.6
  1.3 0.0 copy-start.4
  1.3 0.7 maximum_maximum_fusion.b_in
  2.0 0.0 copy-done.4
  2.0 0.1 copy.23
  2.1 0.1 reshape.43
  2.2 0.2 convert_reduce_fusion
  2.4 0.1 select_reduce_fusion
  2.5 0.6 pad_add_fusion.table
  3.1 0.0 copy-start.1
  3.1 2.2 %copy.24 = bf16[16,2,100,128]{3,2,1,0:T(8,128)(2,1)} copy(bf16[16,2,100,128]{3,1,2,0:T(2,128)(2,1)} %param.7) | data formatting | bytes 1638400 | tf_op args[0]
  5.3 0.0 copy-done.1
  5.3 1.1 %copy.25 = bf16[16,2,100,128]{3,2,1,0:T(8,128)(2,1)} copy(bf16[16,2,100,128]{3,1,2,0:T(2,128)(2,1)S(1)} %copy-done.1) | data formatting | bytes 1638400 | tf_op args[1]
  6.4 77.5 %league.1 = (bf16[32,100,128]{2,1,0:T(8,128)(2,1)}, bf16[32,100,128]{2,1,0:T(8,128)(2,1)}, f32[1,1152,128]{2,1,0:T(8,128)}, f32[1,1152,128]{2,1,0:T(8,128)}, f32[1,128]{1,0:T(1,128)}, /*index=5*/f32[1,128]{1,0:T(1,128)}) custom-call(s32[96]{0:T(128)} %pad_add_fusion.table, bf16[32,100,128]{2,1,0:T(8,128)(2,1)} %bitcast.6, bf16[32,100,128]{2,1,0:T(8,128)(2,1)} %bitcast.7, ...), custom_call_target="tpu_custom_call" | custom-call | flops 11324620800 | bytes 9000000 | tf_op jit(solution)/shard_map/league/pallas_call | solution.py:522
  83.8 0.0 copy-start
  83.9 2.8 %copy.26 = bf16[16,2,100,128]{3,1,2,0:T(2,128)(2,1)} copy(bf16[16,2,100,128]{3,2,1,0:T(8,128)(2,1)} %bitcast.5) | data formatting | bytes 1638400
  86.6 0.0 copy-done
  86.6 0.0 copy-start.3
  86.6 1.5 %copy.27 = bf16[16,2,100,128]{3,1,2,0:T(2,128)(2,1)} copy(bf16[16,2,100,128]{3,2,1,0:T(8,128)(2,1)S(1)} %bitcast.4) | data formatting | bytes 1638400
  88.1 0.0 copy-done.3
  88.1 0.0 copy-start.2
  88.1 0.8 copy.32
  89.0 0.5 copy-done.2
  89.4 0.0 copy-start.8
  89.4 0.8 copy.33
  90.2 0.0 copy-done.8
  90.2 0.0 copy-start.7
  90.2 0.5 copy.34
  90.8 0.1 copy-done.7
  90.8 0.5 copy.35
  (3 shorter events, 0.0 us)
Async XLA Ops:
  0.6 0.7 copy-start.5
  0.7 0.7 copy-start.6
  1.3 0.7 copy-start.4
  3.1 2.2 %copy-start.1 = (bf16[16,2,100,128]{3,1,2,0:T(2,128)(2,1)S(1)}, bf16[16,2,100,128]{3,1,2,0:T(2,128)(2,1)}, u32[]{:S(2)}) copy-start(bf16[16,2,100,128]{3,1,2,0:T(2,128)(2,1)} %param.8) | copy-start | bytes 2457604
  83.8 2.8 %copy-start = (bf16[32,100,128]{2,1,0:T(8,128)(2,1)S(1)}, bf16[32,100,128]{2,1,0:T(8,128)(2,1)}, u32[]{:S(2)}) copy-start(bf16[32,100,128]{2,1,0:T(8,128)(2,1)} %get-tuple-element.13) | copy-start | bytes 2457604
  86.6 1.5 %copy-start.3 = (f32[1,1152,128]{2,1,0:T(8,128)S(1)}, f32[1,1152,128]{2,1,0:T(8,128)}, u32[]{:S(2)}) copy-start(f32[1,1152,128]{2,1,0:T(8,128)} %get-tuple-element.46) | copy-start | bytes 1769476
  88.1 1.3 %copy-start.2 = (f32[1,1152,128]{2,1,0:T(8,128)S(1)}, f32[1,1152,128]{2,1,0:T(8,128)}, u32[]{:S(2)}) copy-start(f32[1,1152,128]{2,1,0:T(8,128)} %get-tuple-element.47) | copy-start | bytes 1769476
  89.4 0.8 copy-start.8
  90.2 0.6 copy-start.7

commit v2 on v1

--- a/solution.py
+++ b/solution.py
@@ -171,10 +171,10 @@
 
 
 def league_kernel(
-    table, acts_in, cot_in, w1_in, w2_in, b_in,
-    out_ref, back_ref, grad_one, grad_two, bias_one, bias_two,
-    acts, cot, w1, w2, bs, xb, gb, hb, pb, slope, mix, res_out, res_back,
-    even, odd, paired, chips, diag, cross, total, split, parts, whole,
+    table, acts_in, cot_in, w1_in, w2_in, b1_in, b2_in,
+    out_ref, back_ref, whole,
+    acts_pair, cot_pair, pair, acts, cot, w1, w2, bs, xb, gb, hb, pb, slope, mix, res_out, res_back,
+    even, odd, paired, chips, diag, cross, total, split, parts,
     load_sems, w_send, w_recv, g_send, g_recv, z_send, z_recv,
 ):
     f32, bf16 = jnp.float32, jnp.bfloat16
@@ -192,7 +192,11 @@
     loads = [
         pltpu.make_async_copy(src, dst, load_sems.at[at])
         for at, (src, dst) in enumerate(
-            ((acts_in, acts), (cot_in, cot), (w1_in.at[0], w1.at[0]), (w2_in.at[0], w2.at[0]), (b_in, bs.at[0]))
+            (
+                (w1_in.at[0], w1.at[0]), (w2_in.at[0], w2.at[0]),
+                (b1_in, bs.at[0, pl.ds(0, 1), :]), (b2_in, bs.at[0, pl.ds(1, 1), :]),
+                (acts_in, acts_pair), (cot_in, cot_pair),
+            )
         )
     ]
     for load in loads:
@@ -208,6 +212,15 @@
         ref[...] = jnp.zeros_like(ref)
     for load in loads:
         load.wait()
+
+    def apart(state, carry):
+        for at, (src, dst) in enumerate(((acts_pair, acts), (cot_pair, cot))):
+            pair[at] = src[state].astype(f32)
+            for side in range(2):
+                dst[state * 2 + side] = pair[at, pl.ds(side, CELLS, stride=2), :].astype(bf16)
+        return carry
+
+    lax.fori_loop(0, acts_pair.shape[0], apart, 0)
     pl.semaphore_wait(barrier, 2 + copies)
 
     def remote(src, dst, sends, recvs, at, peer):
@@ -321,14 +334,8 @@
             rep_copy(j, 1, far).start()
 
     def finish(j):
-        grad, bias = ((grad_one, bias_one), (grad_two, bias_two))[j]
         for far in range(1, copies):
             arrived_rep(j, far).wait_recv()
-        stacked = jnp.concatenate([whole[j, at] for at in range(copies)], axis=0).astype(f32)
-        for tap in range(9):
-            rows = slice(tap * channels, (tap + 1) * channels)
-            grad[0, rows, :] = stacked[rows].T
-        bias[...] = whole[j, copies - 1, quarter - TAIL : quarter - TAIL + 8].astype(f32)[:1]
 
     def patch(board, q):
         columns = []
@@ -473,10 +480,16 @@
     lax.fori_loop(0, len(ORDER), step, 0)
 
     send_whole(0)
-    for row in range(out_ref.shape[0]):
-        at = table[8 * SLOTS + row]
-        out_ref[row] = res_out[at]
-        back_ref[row] = res_back[at]
+
+    def together(state, carry):
+        for at, (src, dst) in enumerate(((res_out, out_ref), (res_back, back_ref))):
+            for side in range(2):
+                row = table[8 * SLOTS + state * 2 + side]
+                pair[at, pl.ds(side, CELLS, stride=2), :] = src[row].astype(f32)
+            dst[state] = pair[at].astype(bf16)
+        return carry
+
+    lax.fori_loop(0, out_ref.shape[0], together, 0)
     finish(1)
     finish(0)
 
@@ -490,6 +503,25 @@
         for stage in range(2):
             for far in range(1, copies):
                 rep_copy(j, stage, far).wait_send()
+
+
+def last_kernel(out_in, back_in, whole, out_ref, back_ref, grad_one, grad_two, bias_one, bias_two, sems):
+    channels = whole.shape[-1]
+    moves = [
+        pltpu.make_async_copy(src, dst, sems.at[at])
+        for at, (src, dst) in enumerate(((out_in, out_ref), (back_in, back_ref)))
+    ]
+    for move in moves:
+        move.start()
+    copies, quarter = whole.shape[1:3]
+    for j, (grad, bias) in enumerate(((grad_one, bias_one), (grad_two, bias_two))):
+        stacked = jnp.concatenate([whole[j, at] for at in range(copies)], axis=0).astype(jnp.float32)
+        for tap in range(9):
+            rows = slice(tap * channels, (tap + 1) * channels)
+            grad[0, rows, :] = stacked[rows].T
+        bias[...] = whole[j, copies - 1, quarter - TAIL : quarter - TAIL + 8].astype(jnp.float32)[:1]
+    for move in moves:
+        move.wait()
 
 
 def at_home(acts, cotangent, routes, w_first, w_second, b_first, b_second):
@@ -508,10 +540,10 @@
     hit = position[None, :] == jnp.arange(owners * SLOTS, dtype=jnp.int32)[:, None]
     rows = jnp.sum(jnp.where(hit, order[None, :] + 1, 0), axis=1) - 1
     table = jnp.concatenate([rows, position])
-    biases = jnp.concatenate([b_first, b_second, jnp.zeros((6, channels), f32)], axis=0)
-
-    x = acts.reshape((count,) + acts.shape[2:])
-    g = cotangent.reshape((count,) + acts.shape[2:])
+    def paired(values):
+        return jnp.swapaxes(values, 1, 2).reshape(values.shape[0], 2 * values.shape[2], channels)
+
+    x, g = paired(acts), paired(cotangent)
     anywhere = pl.BlockSpec(memory_space=pl.ANY)
     vmem = pl.BlockSpec(memory_space=pltpu.VMEM)
     shape = jax.ShapeDtypeStruct
@@ -524,16 +556,16 @@
         out_shape=(
             shape(x.shape, bf16),
             shape(x.shape, bf16),
-            shape((1, taps, channels), f32),
-            shape((1, taps, channels), f32),
-            shape((1, channels), f32),
-            shape((1, channels), f32),
+            shape((2, copies, rows_g // copies, channels), bf16),
         ),
-        in_specs=[pl.BlockSpec(memory_space=pltpu.SMEM)] + [anywhere] * 5,
-        out_specs=(vmem,) * 6,
+        in_specs=[pl.BlockSpec(memory_space=pltpu.SMEM)] + [anywhere] * 6,
+        out_specs=(vmem,) * 3,
         scratch_shapes=[
             pltpu.VMEM(x.shape, bf16),
             pltpu.VMEM(x.shape, bf16),
+            pltpu.VMEM((2, 2 * CELLS, channels), f32),
+            pltpu.VMEM((count, CELLS, channels), bf16),
+            pltpu.VMEM((count, CELLS, channels), bf16),
             weight,
             weight,
             pltpu.VMEM((owners, 8, channels), f32),
@@ -554,8 +586,7 @@
             pltpu.VMEM((2, rows_g, channels), f32),
             pltpu.VMEM((2, rows_g, channels), bf16),
             pltpu.VMEM((2, copies - 1, rows_g // copies, channels), bf16),
-            pltpu.VMEM((2, copies, rows_g // copies, channels), bf16),
-            sems((5,)),
+            sems((6,)),
             sems((24,)),
             sems((24,)),
             sems((16,)),
@@ -570,8 +601,29 @@
             flops=12 * owners * ROWS * taps * channels, bytes_accessed=9000000, transcendentals=owners * ROWS * channels
         ),
         name="league",
-    )(table, x, g, w_first, w_second, biases)
-    return (made[0].reshape(acts.shape), made[1].reshape(acts.shape)) + tuple(made[2:])
+    )(table, x, g, w_first, w_second, b_first, b_second)
+    done = pl.pallas_call(
+        last_kernel,
+        out_shape=(
+            shape(x.shape, bf16),
+            shape(x.shape, bf16),
+            shape((1, taps, channels), f32),
+            shape((1, taps, channels), f32),
+            shape((1, channels), f32),
+            shape((1, channels), f32),
+        ),
+        in_specs=[anywhere] * 2 + [vmem],
+        out_specs=(anywhere,) * 2 + (vmem,) * 4,
+        scratch_shapes=[sems((2,))],
+        compiler_params=pltpu.CompilerParams(vmem_limit_bytes=8 * 1024 * 1024),
+        cost_estimate=pl.CostEstimate(flops=0, bytes_accessed=5000000, transcendentals=0),
+        name="last",
+    )(*made)
+
+    def unpaired(values):
+        return jnp.swapaxes(values.reshape(acts.shape[0], acts.shape[2], 2, channels), 1, 2)
+
+    return (unpaired(done[0]), unpaired(done[1])) + tuple(done[2:])
 
 
 def solution(mesh):

time: 91.1 us -> 84.2 us (0.924)
  local copies, waits for them, and re-layouts: 11.6 us -> 4.2 us
    unnamed x27 -> x9, local copies, waits for them, and re-layouts: 11.5 us -> 4.11 us
    pallas_call x0 -> x1, Pallas kernels: none -> 2.26 us  [at_home(): pl.pallas_call(last_kernel, out_shape=(shape(x.shape, bf16), shape(x.shap...]
    pallas_call x1, Pallas kernels: 77.5 us -> 75.8 us  [at_home(): pl.pallas_call(league_kernel, out_shape=(shape(x.shape, bf16), shape(x.sh...]
where the time goes in v2:
time: 84.2 us; the launch traced here: 83.9 us
  Pallas kernels  78.1 us (93%)
  local copies, waits for them, and re-layouts  4.2 us (5%)
  other arithmetic  0.87 us (1%)
    pallas_call x1, Pallas kernels, at_home(): pl.pallas_call(league_kernel, out_shape=(shape(x.shape, bf16), shape(x.sh...  75.8 us
    unnamed x9, local copies, waits for them, and re-layouts  4.11 us
    pallas_call x1, Pallas kernels, at_home(): pl.pallas_call(last_kernel, out_shape=(shape(x.shape, bf16), shape(x.shap...  2.26 us

profile of v2, /device:TPU:0, one launch (start us, length us, event | category | flops | bytes accessed | tf_op | source)
XLA Modules:
  0.0 83.9 jit_solution(15616458353539365226)
XLA Ops:
  0.6 0.0 copy-start.3
  0.6 0.7 copy-done.3
  1.3 0.1 copy.15
  1.4 0.1 reshape.43
  1.5 0.2 convert_reduce_fusion
  1.7 0.1 select_reduce_fusion
  1.8 0.6 pad_add_fusion.table
  2.4 75.8 %league.1 = (bf16[16,200,128]{2,1,0:T(8,128)(2,1)}, bf16[16,200,128]{2,1,0:T(8,128)(2,1)}, bf16[2,4,304,128]{3,2,1,0:T(8,128)(2,1)}) custom-call(s32[96]{0:T(128)} %pad_add_fusion.table, bf16[16,200,128]{2,1,0:T(8,128)(2,1)} %bitcast.12, bf16[16,200,128]{2,1,0:T(8,128)(2,1)} %bitcast.13, bf16[1,1152,128]{2,1,0:T(8,128)(2,1)} %w1_in.1, ...), custom_call_target="tpu_custom_call" | custom-call | flops 11324620800 | bytes 9000000 | tf_op jit(solution)/shard_map/league/pallas_call | solution.py:554
  78.2 0.0 copy-start
  78.2 1.1 %copy-done = bf16[16,200,128]{2,1,0:T(8,128)(2,1)S(1)} copy-done((bf16[16,200,128]{2,1,0:T(8,128)(2,1)S(1)}, bf16[16,200,128]{2,1,0:T(8,128)(2,1)}, u32[]{:S(2)}) %copy-start) | copy-done | bytes 819224
  79.4 0.0 copy-start.1
  79.4 1.1 %copy-done.1 = bf16[16,200,128]{2,1,0:T(8,128)(2,1)S(1)} copy-done((bf16[16,200,128]{2,1,0:T(8,128)(2,1)S(1)}, bf16[16,200,128]{2,1,0:T(8,128)(2,1)}, u32[]{:S(2)}) %copy-start.1) | copy-done | bytes 819224
  80.5 0.0 copy-start.2
  80.5 1.1 %copy-done.2 = bf16[2,4,304,128]{3,2,1,0:T(8,128)(2,1)S(1)} copy-done((bf16[2,4,304,128]{3,2,1,0:T(8,128)(2,1)S(1)}, bf16[2,4,304,128]{3,2,1,0:T(8,128)(2,1)}, u32[]{:S(2)}) %copy-start.2) | copy-done | bytes 622616
  81.6 2.3 %last.1 = (bf16[16,200,128]{2,1,0:T(8,128)(2,1)}, bf16[16,200,128]{2,1,0:T(8,128)(2,1)}, f32[1,1152,128]{2,1,0:T(8,128)}, f32[1,1152,128]{2,1,0:T(8,128)}, f32[1,128]{1,0:T(1,128)}, /*index=5*/f32[1,128]{1,0:T(1,128)}) custom-call(bf16[16,200,128]{2,1,0:T(8,128)(2,1)S(1)} %copy-done, bf16[16,200,128]{2,1,0:T(8,128)(2,1)S(1)} %copy-done.1, ...), custom_call_target="tpu_custom_call" | custom-call | bytes 5000000 | tf_op jit(solution)/shard_map/last/pallas_call | solution.py:605
  (2 shorter events, 0.0 us)
Async XLA Ops:
  0.6 0.7 copy-start.3
  78.2 1.1 %copy-start = (bf16[16,200,128]{2,1,0:T(8,128)(2,1)S(1)}, bf16[16,200,128]{2,1,0:T(8,128)(2,1)}, u32[]{:S(2)}) copy-start(bf16[16,200,128]{2,1,0:T(8,128)(2,1)} %get-tuple-element.15.out_in) | copy-start | bytes 2457604
  79.4 1.1 %copy-start.1 = (bf16[16,200,128]{2,1,0:T(8,128)(2,1)S(1)}, bf16[16,200,128]{2,1,0:T(8,128)(2,1)}, u32[]{:S(2)}) copy-start(bf16[16,200,128]{2,1,0:T(8,128)(2,1)} %get-tuple-element.16.back_in) | copy-start | bytes 2457604
  80.5 1.1 %copy-start.2 = (bf16[2,4,304,128]{3,2,1,0:T(8,128)(2,1)S(1)}, bf16[2,4,304,128]{3,2,1,0:T(8,128)(2,1)}, u32[]{:S(2)}) copy-start(bf16[2,4,304,128]{3,2,1,0:T(8,128)(2,1)} %get-tuple-element.17.whole) | copy-start | bytes 1867780

commit v3 on v2

--- a/solution.py
+++ b/solution.py
@@ -155,9 +155,9 @@
 MESH_ID = pl.DeviceIdType.MESH
 
 ORDER = (
-    ["A0", "A1", "B0", "C0", "A2", "A4", "A3", "A5", "A6", "A7"]
-    + ["B2", "B4", "C2", "B6", "B7", "B3", "B5", "B1"]
-    + ["C1", "C4", "C3", "C5", "C6", "C7"]
+    ["A0", "A1", "B0", "A2", "A4", "A3", "A6", "A7", "A5"]
+    + ["B2", "B3", "B6", "B7", "B4", "B5", "B1"]
+    + ["C0", "C1", "C2", "C3", "C4", "C5", "C6", "C7"]
 )
 AT = {name: index for index, name in enumerate(ORDER)}
 
@@ -174,19 +174,20 @@
     table, acts_in, cot_in, w1_in, w2_in, b1_in, b2_in,
     out_ref, back_ref, whole,
     acts_pair, cot_pair, pair, acts, cot, w1, w2, bs, xb, gb, hb, pb, slope, mix, res_out, res_back,
-    even, odd, paired, chips, diag, cross, total, split, parts,
+    even, odd, paired, chips, diag, cross, total, split, outside, inside,
     load_sems, w_send, w_recv, g_send, g_recv, z_send, z_recv,
 ):
     f32, bf16 = jnp.float32, jnp.bfloat16
     channels = w1.shape[-1]
     taps = 9 * channels
-    half_w = taps // 2
+    block = taps // 4
     rows_g = taps + TAIL
     half_g = rows_g // 2
-    copies = whole.shape[1]
-    quarter = rows_g // copies
+    quarter = rows_g // 4
     me = lax.axis_index("member")
     rep = lax.axis_index("rep")
+    odd_plane = rep % 2
+    inner_plane = ((rep + 1) // 2) % 2 == 1
     near = {"core": me ^ 1, "x": me ^ 2, "y": me ^ 4}
 
     loads = [
@@ -205,8 +206,163 @@
     barrier = pltpu.get_barrier_semaphore()
     for peer in near.values():
         pl.semaphore_signal(barrier, inc=1, device_id={"member": peer}, device_id_type=MESH_ID)
-    for far in range(1, copies):
+    for far in (1, 3):
         pl.semaphore_signal(barrier, inc=1, device_id={"rep": rep ^ far}, device_id_type=MESH_ID)
+    pl.semaphore_wait(barrier, 5)
+
+    def remote(src, dst, sends, recvs, at, peer):
+        return pltpu.make_async_remote_copy(
+            src_ref=src, dst_ref=dst, send_sem=sends.at[at], recv_sem=recvs.at[at],
+            device_id=peer, device_id_type=MESH_ID,
+        )
+
+    def member(name):
+        return {"member": near[name]}
+
+    def rows_of(at, blocks=1):
+        return pl.ds(pl.multiple_of(at * block, block), blocks * block)
+
+    extra, skipped = 1 + 2 * odd_plane, 3 - 2 * odd_plane
+    lead, other = 2 * odd_plane, 2 - 2 * odd_plane
+    plane = {"rep": rep ^ 1}
+
+    def give(kind, at, arriving=False):
+        buffer = (w1, w2)[kind]
+        own = (w1_in, w2_in)[kind].at[0]
+        if at in (0, 12, 13, 14):
+            src, dst = {0: (own, 1), 12: (buffer.at[2], 3), 13: (buffer.at[4], 5), 14: (buffer.at[6], 7)}[at]
+            ends = (src, buffer.at[dst], member("core"))
+        elif at < 7:
+            rows = rows_of((extra, lead, other)[(at - 1) % 3])
+            to = 2 if at < 4 else 4
+            ends = (own.at[rows, :], buffer.at[to, rows, :], member("x" if at < 4 else "y"))
+        elif at < 9:
+            to = 2 * (at - 6)
+            target = buffer.at[to, rows_of(skipped if arriving else extra), :]
+            ends = (buffer.at[to, rows_of(extra), :], target, plane)
+        elif at == 9:
+            ends = (buffer.at[2, rows_of(lead), :], buffer.at[6, rows_of(lead), :], member("y"))
+        elif at == 10:
+            ends = (buffer.at[4, rows_of(extra), :], buffer.at[6, rows_of(extra), :], member("x"))
+        else:
+            target = buffer.at[6, rows_of(other if arriving else lead, 2), :]
+            ends = (buffer.at[6, rows_of(lead, 2), :], target, plane)
+        return remote(ends[0], ends[1], w_send, w_recv, kind * 16 + at, ends[2])
+
+    def give_bias(at):
+        src, dst, peer = (
+            (0, 1, "core"), (0, 2, "x"), (0, 4, "y"), (2, 3, "core"), (4, 5, "core"), (2, 6, "y"), (6, 7, "core")
+        )[at]
+        return remote(bs.at[src], bs.at[dst], w_send, w_recv, 32 + at, member(peer))
+
+    def send_weights(kind, ats):
+        for at in ats:
+            give(kind, at).start()
+
+    def have_weights(kind, ats):
+        for at in ats:
+            give(kind, at, True).wait_recv()
+
+    def send_bias(*ats):
+        for at in ats:
+            give_bias(at).start()
+
+    def have_bias(*ats):
+        for at in ats:
+            give_bias(at).wait_recv()
+
+    def grad_copy(j, at):
+        if at < 4:
+            ends = (odd.at[j, at], paired.at[j, at], "core")
+        elif at < 6:
+            rows = pl.ds((at - 4) * half_g, half_g)
+            ends = (chips.at[j, 3, rows, :], diag.at[j, at - 4], "xy"[at - 4])
+        else:
+            p, c = (at - 6) // 4, (at - 6) % 4
+            rows = pl.ds(c * quarter, quarter)
+            ends = (chips.at[j, p + 1, rows, :], cross.at[j, p, rows, :], "xy"[p])
+        return remote(ends[0], ends[1], g_send, g_recv, j * 16 + at, member(ends[2]))
+
+    def rep_copy(j, stage, c):
+        src, dst, far = (
+            (split.at[j, c], outside.at[j, c], 1),
+            (split.at[j, c], inside.at[j, c], 3),
+            (whole.at[j, c], whole.at[j, c], 1),
+        )[stage]
+        return remote(src, dst, z_send, z_recv, (j * 3 + stage) * 4 + c, {"rep": rep ^ far})
+
+    def send_pair(j, p):
+        grad_copy(j, p).start()
+
+    def send_diag(j):
+        grad_copy(j, 3).wait_recv()
+        chips[j, 3] = (even[j, 3] + paired[j, 3].astype(f32)).astype(bf16)
+        grad_copy(j, 4).start()
+        grad_copy(j, 5).start()
+
+    def send_free(j, p):
+        grad_copy(j, p).wait_recv()
+        rows = slice(0, half_g) if p == 1 else slice(half_g, rows_g)
+        chips[j, p, rows] = (even[j, p, rows] + paired[j, p, rows].astype(f32)).astype(bf16)
+        for c in ((0, 1) if p == 1 else (2, 3)):
+            grad_copy(j, 6 + 4 * (p - 1) + c).start()
+
+    def send_rest(j, p):
+        grad_copy(j, 6 - p).wait_recv()
+        rows = slice(half_g, rows_g) if p == 1 else slice(0, half_g)
+        value = even[j, p, rows] + paired[j, p, rows].astype(f32) + diag[j, 2 - p].astype(f32)
+        chips[j, p, rows] = value.astype(bf16)
+        for c in ((2, 3) if p == 1 else (0, 1)):
+            grad_copy(j, 6 + 4 * (p - 1) + c).start()
+
+    def have_own(j):
+        grad_copy(j, 0).wait_recv()
+
+    def add_up(j, *cs):
+        for c in cs:
+            rows = slice(c * quarter, (c + 1) * quarter)
+            grad_copy(j, 6 + c).wait_recv()
+            grad_copy(j, 10 + c).wait_recv()
+            value = even[j, 0, rows] + paired[j, 0, rows].astype(f32)
+            total[j, c] = value + cross[j, 0, rows].astype(f32) + cross[j, 1, rows].astype(f32)
+
+            @pl.when(jnp.logical_not(inner_plane))
+            def _():
+                split[j, c] = total[j, c].astype(bf16)
+                rep_copy(j, 0, c).start()
+
+    def middle(j, *cs):
+        @pl.when(inner_plane)
+        def _():
+            for c in cs:
+                rep_copy(j, 0, c).wait_recv()
+                split[j, c] = (total[j, c] + outside[j, c].astype(f32)).astype(bf16)
+                rep_copy(j, 1, c).start()
+
+    def ending(j, *cs):
+        @pl.when(inner_plane)
+        def _():
+            for c in cs:
+                rep_copy(j, 1, c).wait_recv()
+                whole[j, c] = (split[j, c].astype(f32) + inside[j, c].astype(f32)).astype(bf16)
+                rep_copy(j, 2, c).start()
+
+    def settle():
+        @pl.when(jnp.logical_not(inner_plane))
+        def _():
+            for j in range(2):
+                for c in range(4):
+                    rep_copy(j, 2, c).wait_recv()
+                    rep_copy(j, 0, c).wait_send()
+
+        @pl.when(inner_plane)
+        def _():
+            for j in range(2):
+                for c in range(4):
+                    rep_copy(j, 1, c).wait_send()
+                    rep_copy(j, 2, c).wait_send()
+
+    send_weights(0, (1, 4, 2, 5, 3, 6, 0))
 
     for ref in (xb, gb, hb, pb):
         ref[...] = jnp.zeros_like(ref)
@@ -221,121 +377,6 @@
         return carry
 
     lax.fori_loop(0, acts_pair.shape[0], apart, 0)
-    pl.semaphore_wait(barrier, 2 + copies)
-
-    def remote(src, dst, sends, recvs, at, peer):
-        return pltpu.make_async_remote_copy(
-            src_ref=src, dst_ref=dst, send_sem=sends.at[at], recv_sem=recvs.at[at],
-            device_id=peer, device_id_type=MESH_ID,
-        )
-
-    def member(name):
-        return {"member": near[name]}
-
-    low, high = pl.ds(0, half_w), pl.ds(half_w, taps - half_w)
-
-    def give(kind, at):
-        buffer = (w1, w2, bs)[kind]
-        moves = [
-            (0, 1, None, "core"), (0, 2, None, "x"), (0, 4, None, "y"),
-            (2, 3, None, "core"), (4, 5, None, "core"),
-            (2, 6, low, "y"), (4, 6, high, "x"), (6, 7, None, "core"),
-        ]
-        src, dst, rows, peer = moves[at]
-        if kind == 2 or rows is None:
-            pair = (buffer.at[src], buffer.at[dst])
-        else:
-            pair = (buffer.at[src, rows, :], buffer.at[dst, rows, :])
-        return remote(pair[0], pair[1], w_send, w_recv, kind * 8 + at, member(peer))
-
-    def biases(ats):
-        return [at for at in ats if at != 6]
-
-    def send_weights(kind, ats):
-        for at in ats:
-            give(kind, at).start()
-        if kind == 0:
-            for at in biases(ats):
-                give(2, at).start()
-
-    def have_weights(kind, ats):
-        for at in ats:
-            give(kind, at).wait_recv()
-        if kind == 0:
-            for at in biases(ats):
-                give(2, at).wait_recv()
-
-    first, second = pl.ds(0, half_g), pl.ds(half_g, half_g)
-
-    def grad_copy(j, at):
-        if at < 4:
-            return remote(odd.at[j, at], paired.at[j, at], g_send, g_recv, j * 8 + at, member("core"))
-        if at == 4:
-            return remote(chips.at[j, 3, first, :], diag.at[j, 0], g_send, g_recv, j * 8 + 4, member("x"))
-        if at == 5:
-            return remote(chips.at[j, 3, second, :], diag.at[j, 1], g_send, g_recv, j * 8 + 5, member("y"))
-        return remote(
-            chips.at[j, at - 5], cross.at[j, at - 6], g_send, g_recv, j * 8 + at, member("x" if at == 6 else "y")
-        )
-
-    def rep_copy(j, stage, far):
-        at = (j * 2 + stage) * copies + far
-        peer = {"rep": rep ^ far}
-        if stage == 0:
-            return remote(
-                split.at[j, pl.ds((rep ^ far) * quarter, quarter), :], parts.at[j, far - 1], z_send, z_recv, at, peer
-            )
-        return remote(whole.at[j, rep], whole.at[j, rep], z_send, z_recv, at, peer)
-
-    def arrived_rep(j, far):
-        return remote(
-            whole.at[j, rep], whole.at[j, rep ^ far], z_send, z_recv, (j * 2 + 1) * copies + far, {"rep": rep ^ far}
-        )
-
-    def pair_up(j, p):
-        grad_copy(j, p).wait_recv()
-        return even[j, p] + paired[j, p].astype(f32)
-
-    def send_diag(j):
-        chips[j, 3] = pair_up(j, 3).astype(bf16)
-        grad_copy(j, 4).start()
-        grad_copy(j, 5).start()
-
-    def send_cross(j, p):
-        value = pair_up(j, p)
-        if p == 1:
-            grad_copy(j, 5).wait_recv()
-            chips[j, 1, :half_g] = value[:half_g].astype(bf16)
-            chips[j, 1, half_g:] = (value[half_g:] + diag[j, 1].astype(f32)).astype(bf16)
-            grad_copy(j, 6).start()
-        else:
-            grad_copy(j, 4).wait_recv()
-            chips[j, 2, :half_g] = (value[:half_g] + diag[j, 0].astype(f32)).astype(bf16)
-            chips[j, 2, half_g:] = value[half_g:].astype(bf16)
-            grad_copy(j, 7).start()
-
-    def send_split(j):
-        value = pair_up(j, 0)
-        grad_copy(j, 6).wait_recv()
-        grad_copy(j, 7).wait_recv()
-        value = value + cross[j, 0].astype(f32) + cross[j, 1].astype(f32)
-        total[j] = value
-        split[j] = value.astype(bf16)
-        for far in range(1, copies):
-            rep_copy(j, 0, far).start()
-
-    def send_whole(j):
-        mine = total[j, pl.ds(rep * quarter, quarter), :]
-        for far in range(1, copies):
-            rep_copy(j, 0, far).wait_recv()
-            mine = mine + parts[j, far - 1].astype(f32)
-        whole[j, rep] = mine.astype(bf16)
-        for far in range(1, copies):
-            rep_copy(j, 1, far).start()
-
-    def finish(j):
-        for far in range(1, copies):
-            arrived_rep(j, far).wait_recv()
 
     def patch(board, q):
         columns = []
@@ -420,39 +461,62 @@
     def on(name, action, *args):
         before[name].append(functools.partial(action, *args))
 
-    send_weights(0, (1, 2, 0))
+    send_bias(0, 1, 2)
     on("A1", have_weights, 0, (0,))
-    on("A2", have_weights, 0, (1, 2))
-    on("A2", send_weights, 0, (5, 6, 3, 4))
-    on("A2", send_weights, 1, (1, 2, 0))
-    on("A3", have_weights, 0, (3,))
-    on("A5", have_weights, 0, (4,))
-    on("A6", have_weights, 0, (5, 6))
-    on("A6", send_weights, 0, (7,))
-    on("A7", have_weights, 0, (7,))
-    on("B2", have_weights, 1, (1, 2))
-    on("B2", send_weights, 1, (5, 6, 3, 4))
-    on("B6", have_weights, 1, (5, 6))
-    on("B6", send_weights, 1, (7,))
-    on("B7", have_weights, 1, (7,))
-    on("B3", have_weights, 1, (3,))
-    on("B5", have_weights, 1, (4,))
+    on("A1", have_bias, 0)
+    on("B0", have_weights, 0, (1, 2, 4))
+    on("B0", send_weights, 0, (9, 10, 7, 8))
+    on("B0", send_weights, 1, (1, 4, 2, 5, 3, 6, 0))
+    on("A2", have_weights, 0, (3, 7, 5, 6, 8))
+    on("A2", send_weights, 0, (12, 13))
+    on("A2", have_bias, 1, 2)
+    on("A2", send_bias, 3, 4, 5)
+    on("A4", have_weights, 0, (9, 10))
+    on("A4", send_weights, 0, (11,))
+    on("A3", have_weights, 0, (12,))
+    on("A3", have_bias, 3)
+    on("A6", have_weights, 0, (11,))
+    on("A6", send_weights, 0, (14,))
+    on("A6", have_bias, 5)
+    on("A6", send_bias, 6)
+    on("A6", have_weights, 1, (1, 2, 4))
+    on("A6", send_weights, 1, (9, 10, 7, 8))
+    on("A7", have_weights, 0, (14,))
+    on("A7", have_bias, 6)
+    on("A5", have_weights, 0, (13,))
+    on("A5", have_bias, 4)
+    on("A5", have_weights, 1, (9, 10))
+    on("A5", send_weights, 1, (11,))
+    on("A5", have_weights, 1, (3, 7, 5, 6, 8))
+    on("A5", send_weights, 1, (12, 13))
+    on("B3", have_weights, 1, (12,))
+    on("B6", have_weights, 1, (11,))
+    on("B6", send_weights, 1, (14,))
+    on("B7", have_weights, 1, (14,))
+    on("B5", have_weights, 1, (13,))
     on("B1", have_weights, 1, (0,))
 
     for j, phase in ((1, "A"), (0, "B")):
         for p in range(4):
-            done = AT[phase + str(2 * p + 1)]
-            on(ORDER[done + 1], lambda j=j, p=p: grad_copy(j, p).start())
-
-    on("B4", send_diag, 1)
-    on("B6", send_cross, 1, 1)
-    on("B6", send_cross, 1, 2)
+            on(ORDER[AT[phase + str(2 * p + 1)] + 1], send_pair, j, p)
+
+    on("B2", send_diag, 1)
+    on("B6", send_free, 1, 1)
+    on("B6", send_free, 1, 2)
+    on("B7", send_rest, 1, 1)
+    on("B7", send_rest, 1, 2)
     on("B5", send_diag, 0)
-    on("C1", send_split, 1)
-    on("C1", send_cross, 0, 1)
-    on("C4", send_cross, 0, 2)
-    on("C5", send_whole, 1)
-    on("C7", send_split, 0)
+    on("C0", have_own, 1)
+    on("C0", add_up, 1, 0, 2)
+    on("C1", send_free, 0, 1)
+    on("C1", send_free, 0, 2)
+    on("C1", add_up, 1, 1, 3)
+    on("C2", middle, 1, 0, 2)
+    on("C3", send_rest, 0, 1)
+    on("C3", send_rest, 0, 2)
+    on("C3", middle, 1, 1, 3)
+    on("C4", ending, 1, 0, 2)
+    on("C5", ending, 1, 1, 3)
 
     phases = {"A": phase_a, "B": phase_b, "C": phase_c}
 
@@ -479,7 +543,6 @@
 
     lax.fori_loop(0, len(ORDER), step, 0)
 
-    send_whole(0)
 
     def together(state, carry):
         for at, (src, dst) in enumerate(((res_out, out_ref), (res_back, back_ref))):
@@ -490,19 +553,23 @@
         return carry
 
     lax.fori_loop(0, out_ref.shape[0], together, 0)
-    finish(1)
-    finish(0)
-
-    for kind in range(3):
-        for at in range(8):
-            if kind < 2 or at != 6:
-                give(kind, at).wait_send()
+    have_own(0)
+    add_up(0, 0, 2)
+    middle(0, 0, 2)
+    add_up(0, 1, 3)
+    ending(0, 0, 2)
+    middle(0, 1, 3)
+    ending(0, 1, 3)
+    settle()
+
+    for at in range(15):
+        give(0, at).wait_send()
+        give(1, at).wait_send()
+    for at in range(7):
+        give_bias(at).wait_send()
     for j in range(2):
-        for at in range(8):
+        for at in range(14):
             grad_copy(j, at).wait_send()
-        for stage in range(2):
-            for far in range(1, copies):
-                rep_copy(j, stage, far).wait_send()
 
 
 def last_kernel(out_in, back_in, whole, out_ref, back_ref, grad_one, grad_two, bias_one, bias_two, sems):
@@ -513,20 +580,19 @@
     ]
     for move in moves:
         move.start()
-    copies, quarter = whole.shape[1:3]
+    chunks, quarter = whole.shape[1:3]
     for j, (grad, bias) in enumerate(((grad_one, bias_one), (grad_two, bias_two))):
-        stacked = jnp.concatenate([whole[j, at] for at in range(copies)], axis=0).astype(jnp.float32)
+        stacked = jnp.concatenate([whole[j, at] for at in range(chunks)], axis=0).astype(jnp.float32)
         for tap in range(9):
             rows = slice(tap * channels, (tap + 1) * channels)
             grad[0, rows, :] = stacked[rows].T
-        bias[...] = whole[j, copies - 1, quarter - TAIL : quarter - TAIL + 8].astype(jnp.float32)[:1]
+        bias[...] = whole[j, chunks - 1, quarter - TAIL : quarter - TAIL + 8].astype(jnp.float32)[:1]
     for move in moves:
         move.wait()
 
 
 def at_home(acts, cotangent, routes, w_first, w_second, b_first, b_second):
     owners = lax.axis_size("member")
-    copies = lax.axis_size("rep")
     channels = acts.shape[-1]
     taps = 9 * channels
     rows_g = taps + TAIL
@@ -556,7 +622,7 @@
         out_shape=(
             shape(x.shape, bf16),
             shape(x.shape, bf16),
-            shape((2, copies, rows_g // copies, channels), bf16),
+            shape((2, 4, rows_g // 4, channels), bf16),
         ),
         in_specs=[pl.BlockSpec(memory_space=pltpu.SMEM)] + [anywhere] * 6,
         out_specs=(vmem,) * 3,
@@ -583,16 +649,17 @@
             pltpu.VMEM((2, 4, rows_g, channels), bf16),
             pltpu.VMEM((2, 2, rows_g // 2, channels), bf16),
             pltpu.VMEM((2, 2, rows_g, channels), bf16),
-            pltpu.VMEM((2, rows_g, channels), f32),
-            pltpu.VMEM((2, rows_g, channels), bf16),
-            pltpu.VMEM((2, copies - 1, rows_g // copies, channels), bf16),
+            pltpu.VMEM((2, 4, rows_g // 4, channels), f32),
+            pltpu.VMEM((2, 4, rows_g // 4, channels), bf16),
+            pltpu.VMEM((2, 4, rows_g // 4, channels), bf16),
+            pltpu.VMEM((2, 4, rows_g // 4, channels), bf16),
             sems((6,)),
+            sems((40,)),
+            sems((40,)),
+            sems((32,)),
+            sems((32,)),
             sems((24,)),
             sems((24,)),
-            sems((16,)),
-            sems((16,)),
-            sems((4 * copies,)),
-            sems((4 * copies,)),
         ],
         compiler_params=pltpu.CompilerParams(
             collective_id=0, has_side_effects=True, vmem_limit_bytes=60 * 1024 * 1024
@@ -615,7 +682,7 @@
         in_specs=[anywhere] * 2 + [vmem],
         out_specs=(anywhere,) * 2 + (vmem,) * 4,
         scratch_shapes=[sems((2,))],
-        compiler_params=pltpu.CompilerParams(vmem_limit_bytes=8 * 1024 * 1024),
+        compiler_params=pltpu.CompilerParams(vmem_limit_bytes=60 * 1024 * 1024),
         cost_estimate=pl.CostEstimate(flops=0, bytes_accessed=5000000, transcendentals=0),
         name="last",
     )(*made)

time: 84.2 us -> 130 us (1.54)
  Pallas kernels: 78.1 us -> 127 us
  local copies, waits for them, and re-layouts: 4.2 us -> 0.84 us
    pallas_call x1, Pallas kernels: 2.26 us -> 52.8 us  [at_home(): pl.pallas_call(last_kernel, out_shape=(shape(x.shape, bf16), shape(x.shap...]
    unnamed x9 -> x3, local copies, waits for them, and re-layouts: 4.11 us -> 0.75 us
    pallas_call x1, Pallas kernels: 75.8 us -> 74.5 us  [at_home(): pl.pallas_call(league_kernel, out_shape=(shape(x.shape, bf16), shape(x.sh...]
where the time goes in v3:
time: 130 us
  Pallas kernels  127 us (98%)
    pallas_call x1, Pallas kernels, at_home(): pl.pallas_call(league_kernel, out_shape=(shape(x.shape, bf16), shape(x.sh...  74.5 us
    pallas_call x1, Pallas kernels, at_home(): pl.pallas_call(last_kernel, out_shape=(shape(x.shape, bf16), shape(x.shap...  52.8 us

profile of v3, /device:TPU:0, one launch (start us, length us, event | category | flops | bytes accessed | tf_op | source)
XLA Modules:
  0.0 129.7 jit_solution(11594253159123576912)
XLA Ops:
  0.6 0.0 copy-start
  0.6 0.7 copy-done
  1.3 0.1 copy.15
  1.4 0.1 reshape.43
  1.5 0.2 convert_reduce_fusion
  1.7 0.1 select_reduce_fusion
  1.8 0.6 pad_add_fusion.table
  2.4 74.5 %league.1 = (bf16[16,200,128]{2,1,0:T(8,128)(2,1)}, bf16[16,200,128]{2,1,0:T(8,128)(2,1)}, bf16[2,4,304,128]{3,2,1,0:T(8,128)(2,1)}) custom-call(s32[96]{0:T(128)} %pad_add_fusion.table, bf16[16,200,128]{2,1,0:T(8,128)(2,1)} %bitcast.12, bf16[16,200,128]{2,1,0:T(8,128)(2,1)} %bitcast.13, bf16[1,1152,128]{2,1,0:T(8,128)(2,1)} %w1_in.1, ...), custom_call_target="tpu_custom_call" | custom-call | flops 11324620800 | bytes 9000000 | tf_op jit(solution)/shard_map/league/pallas_call | solution.py:620
  76.8 52.8 %last.1 = (bf16[16,200,128]{2,1,0:T(8,128)(2,1)}, bf16[16,200,128]{2,1,0:T(8,128)(2,1)}, f32[1,1152,128]{2,1,0:T(8,128)}, f32[1,1152,128]{2,1,0:T(8,128)}, f32[1,128]{1,0:T(1,128)}, /*index=5*/f32[1,128]{1,0:T(1,128)}) custom-call(bf16[16,200,128]{2,1,0:T(8,128)(2,1)} %get-tuple-element.15.out_in, bf16[16,200,128]{2,1,0:T(8,128)(2,1)} %get-tuple-element.16.back_in, ...), custom_call_target="tpu_custom_call" | custom-call | bytes 5000000 | tf_op jit(solution)/shard_map/last/pallas_call | solution.py:672
  (2 shorter events, 0.0 us)
Async XLA Ops:
  0.6 0.7 copy-start

commit v4 on v3

--- a/solution.py
+++ b/solution.py
@@ -155,9 +155,9 @@
 MESH_ID = pl.DeviceIdType.MESH
 
 ORDER = (
-    ["A0", "A1", "B0", "A2", "A4", "A3", "A6", "A7", "A5"]
-    + ["B2", "B3", "B6", "B7", "B4", "B5", "B1"]
-    + ["C0", "C1", "C2", "C3", "C4", "C5", "C6", "C7"]
+    ["A0", "A1", "B0", "B1", "C0", "D0", "C1", "D1", "A6", "A7", "A2", "A3", "A4", "A5"]
+    + ["B2", "B3", "B6", "B7", "B4", "B5"]
+    + ["C2", "D2", "C3", "D3", "C4", "D4", "C5", "D5", "C6", "D6", "C7", "D7"]
 )
 AT = {name: index for index, name in enumerate(ORDER)}
 
@@ -180,13 +180,12 @@
     f32, bf16 = jnp.float32, jnp.bfloat16
     channels = w1.shape[-1]
     taps = 9 * channels
-    block = taps // 4
+    half_w = taps // 2
     rows_g = taps + TAIL
     half_g = rows_g // 2
     quarter = rows_g // 4
     me = lax.axis_index("member")
     rep = lax.axis_index("rep")
-    odd_plane = rep % 2
     inner_plane = ((rep + 1) // 2) % 2 == 1
     near = {"core": me ^ 1, "x": me ^ 2, "y": me ^ 4}
 
@@ -219,34 +218,20 @@
     def member(name):
         return {"member": near[name]}
 
-    def rows_of(at, blocks=1):
-        return pl.ds(pl.multiple_of(at * block, block), blocks * block)
-
-    extra, skipped = 1 + 2 * odd_plane, 3 - 2 * odd_plane
-    lead, other = 2 * odd_plane, 2 - 2 * odd_plane
-    plane = {"rep": rep ^ 1}
-
-    def give(kind, at, arriving=False):
+    def give(kind, at):
         buffer = (w1, w2)[kind]
         own = (w1_in, w2_in)[kind].at[0]
-        if at in (0, 12, 13, 14):
-            src, dst = {0: (own, 1), 12: (buffer.at[2], 3), 13: (buffer.at[4], 5), 14: (buffer.at[6], 7)}[at]
+        if at in (0, 7, 8, 9):
+            src, dst = {0: (own, 1), 7: (buffer.at[2], 3), 8: (buffer.at[4], 5), 9: (buffer.at[6], 7)}[at]
             ends = (src, buffer.at[dst], member("core"))
-        elif at < 7:
-            rows = rows_of((extra, lead, other)[(at - 1) % 3])
-            to = 2 if at < 4 else 4
-            ends = (own.at[rows, :], buffer.at[to, rows, :], member("x" if at < 4 else "y"))
-        elif at < 9:
-            to = 2 * (at - 6)
-            target = buffer.at[to, rows_of(skipped if arriving else extra), :]
-            ends = (buffer.at[to, rows_of(extra), :], target, plane)
-        elif at == 9:
-            ends = (buffer.at[2, rows_of(lead), :], buffer.at[6, rows_of(lead), :], member("y"))
-        elif at == 10:
-            ends = (buffer.at[4, rows_of(extra), :], buffer.at[6, rows_of(extra), :], member("x"))
+        elif at < 5:
+            rows = pl.ds((0, 1, 1, 0)[at - 1] * half_w, half_w)
+            to = 2 if at < 3 else 4
+            ends = (own.at[rows, :], buffer.at[to, rows, :], member("x" if at < 3 else "y"))
         else:
-            target = buffer.at[6, rows_of(other if arriving else lead, 2), :]
-            ends = (buffer.at[6, rows_of(lead, 2), :], target, plane)
+            source, peer = ((2, "y"), (4, "x"))[at - 5]
+            rows = pl.ds((at - 5) * half_w, half_w)
+            ends = (buffer.at[source, rows, :], buffer.at[6, rows, :], member(peer))
         return remote(ends[0], ends[1], w_send, w_recv, kind * 16 + at, ends[2])
 
     def give_bias(at):
@@ -261,7 +246,7 @@
 
     def have_weights(kind, ats):
         for at in ats:
-            give(kind, at, True).wait_recv()
+            give(kind, at).wait_recv()
 
     def send_bias(*ats):
         for at in ats:
@@ -273,7 +258,7 @@
 
     def grad_copy(j, at):
         if at < 4:
-            ends = (odd.at[j, at], paired.at[j, at], "core")
+            ends = (odd.at[j, 2 * at + 1], paired.at[j, at], "core")
         elif at < 6:
             rows = pl.ds((at - 4) * half_g, half_g)
             ends = (chips.at[j, 3, rows, :], diag.at[j, at - 4], "xy"[at - 4])
@@ -296,21 +281,21 @@
 
     def send_diag(j):
         grad_copy(j, 3).wait_recv()
-        chips[j, 3] = (even[j, 3] + paired[j, 3].astype(f32)).astype(bf16)
+        chips[j, 3] = (even[j, 6] + paired[j, 3].astype(f32)).astype(bf16)
         grad_copy(j, 4).start()
         grad_copy(j, 5).start()
 
     def send_free(j, p):
         grad_copy(j, p).wait_recv()
         rows = slice(0, half_g) if p == 1 else slice(half_g, rows_g)
-        chips[j, p, rows] = (even[j, p, rows] + paired[j, p, rows].astype(f32)).astype(bf16)
+        chips[j, p, rows] = (even[j, 2 * p, rows] + paired[j, p, rows].astype(f32)).astype(bf16)
         for c in ((0, 1) if p == 1 else (2, 3)):
             grad_copy(j, 6 + 4 * (p - 1) + c).start()
 
     def send_rest(j, p):
         grad_copy(j, 6 - p).wait_recv()
         rows = slice(half_g, rows_g) if p == 1 else slice(0, half_g)
-        value = even[j, p, rows] + paired[j, p, rows].astype(f32) + diag[j, 2 - p].astype(f32)
+        value = even[j, 2 * p, rows] + paired[j, p, rows].astype(f32) + diag[j, 2 - p].astype(f32)
         chips[j, p, rows] = value.astype(bf16)
         for c in ((2, 3) if p == 1 else (0, 1)):
             grad_copy(j, 6 + 4 * (p - 1) + c).start()
@@ -362,10 +347,9 @@
                     rep_copy(j, 1, c).wait_send()
                     rep_copy(j, 2, c).wait_send()
 
-    send_weights(0, (1, 4, 2, 5, 3, 6, 0))
-
-    for ref in (xb, gb, hb, pb):
-        ref[...] = jnp.zeros_like(ref)
+    send_weights(0, (1, 3, 2, 4, 0))
+    send_weights(1, (0,))
+
     for load in loads:
         load.wait()
 
@@ -390,6 +374,7 @@
         return jnp.concatenate(columns, axis=1)
 
     def put(board, q, value):
+        board[q] = jnp.zeros_like(board[q])
         for line in range(BOARD):
             board[q, inner(line) : inner(line) + LINE, :] = value[line * LINE : (line + 1) * LINE].astype(bf16)
 
@@ -403,41 +388,31 @@
             [weight[q, (8 - tap) * channels : (9 - tap) * channels, :] for tap in range(9)], axis=1
         )
 
-    def gather(src, board, q):
+    def gather(src, board, q, at):
         for slot in range(SLOTS):
             row = table[q * SLOTS + slot]
             value = src[jnp.maximum(row, 0)].astype(f32)
-            mix[pl.ds(slot, CELLS, stride=SLOTS), :] = jnp.where(row >= 0, value, 0.0)
-        put(board, q, mix[...])
+            mix[at, pl.ds(slot, CELLS, stride=SLOTS), :] = jnp.where(row >= 0, value, 0.0)
+        put(board, q, mix[at])
 
     def spread(ref, q, value):
-        mix[...] = value
+        mix[0] = value
         for slot in range(SLOTS):
-            ref[q * SLOTS + slot] = mix[pl.ds(slot, CELLS, stride=SLOTS), :].astype(bf16)
+            ref[q * SLOTS + slot] = mix[0, pl.ds(slot, CELLS, stride=SLOTS), :].astype(bf16)
 
     def keep_grad(j, q, grad, patches):
         turned = jnp.dot(grad.T.astype(bf16), patches, preferred_element_type=f32)
         bias = jnp.broadcast_to(jnp.sum(grad, axis=0, keepdims=True), (TAIL, channels))
-        pair = q // 2
-
-        def write(ref, kind):
+        for ref in (even, odd):
             for tap in range(9):
-                ref[j, pair, tap * channels : (tap + 1) * channels, :] = turned[
+                ref[j, q, tap * channels : (tap + 1) * channels, :] = turned[
                     :, tap * channels : (tap + 1) * channels
-                ].astype(kind)
-            ref[j, pair, taps:, :] = bias.astype(kind)
-
-        @pl.when(q % 2 == 0)
-        def _():
-            write(even, f32)
-
-        @pl.when(q % 2 == 1)
-        def _():
-            write(odd, bf16)
+                ].astype(ref.dtype)
+            ref[j, q, taps:, :] = bias.astype(ref.dtype)
 
     def phase_a(q):
-        gather(acts, xb, q)
-        gather(cot, gb, q)
+        gather(acts, xb, q, 0)
+        gather(cot, gb, q, 1)
         pre = jnp.dot(patch(xb, q), w1[q], preferred_element_type=f32) + bs[q, 0:1]
         gate = 0.5 * jnp.tanh(0.5 * pre) + 0.5
         slope[q] = gate * (1.0 + pre * (1.0 - gate))
@@ -454,6 +429,8 @@
             res_out, q,
             jnp.dot(patch(hb, q), w2[q], preferred_element_type=f32) + bs[q, 1:2] + centre(xb, q),
         )
+
+    def phase_d(q):
         spread(res_back, q, wide(patch(pb, q), flipped_wide(w1, q)) + centre(gb, q))
 
     before = {name: [] for name in ORDER}
@@ -464,68 +441,67 @@
     send_bias(0, 1, 2)
     on("A1", have_weights, 0, (0,))
     on("A1", have_bias, 0)
-    on("B0", have_weights, 0, (1, 2, 4))
-    on("B0", send_weights, 0, (9, 10, 7, 8))
-    on("B0", send_weights, 1, (1, 4, 2, 5, 3, 6, 0))
-    on("A2", have_weights, 0, (3, 7, 5, 6, 8))
-    on("A2", send_weights, 0, (12, 13))
-    on("A2", have_bias, 1, 2)
-    on("A2", send_bias, 3, 4, 5)
-    on("A4", have_weights, 0, (9, 10))
-    on("A4", send_weights, 0, (11,))
-    on("A3", have_weights, 0, (12,))
-    on("A3", have_bias, 3)
-    on("A6", have_weights, 0, (11,))
-    on("A6", send_weights, 0, (14,))
+    on("B1", have_weights, 1, (0,))
+    on("B1", have_weights, 0, (1, 3))
+    on("B1", send_weights, 0, (5, 6))
+    on("B1", have_weights, 0, (2, 4))
+    on("B1", send_weights, 0, (7, 8))
+    on("B1", have_bias, 1, 2)
+    on("B1", send_bias, 3, 4, 5)
+    on("B1", send_weights, 1, (1, 3, 2, 4))
+    on("A6", have_weights, 0, (5, 6))
+    on("A6", send_weights, 0, (9,))
     on("A6", have_bias, 5)
     on("A6", send_bias, 6)
-    on("A6", have_weights, 1, (1, 2, 4))
-    on("A6", send_weights, 1, (9, 10, 7, 8))
-    on("A7", have_weights, 0, (14,))
+    on("A7", have_weights, 0, (9,))
     on("A7", have_bias, 6)
-    on("A5", have_weights, 0, (13,))
+    on("A3", have_weights, 0, (7,))
+    on("A3", have_bias, 3)
+    on("A5", have_weights, 0, (8,))
     on("A5", have_bias, 4)
-    on("A5", have_weights, 1, (9, 10))
-    on("A5", send_weights, 1, (11,))
-    on("A5", have_weights, 1, (3, 7, 5, 6, 8))
-    on("A5", send_weights, 1, (12, 13))
-    on("B3", have_weights, 1, (12,))
-    on("B6", have_weights, 1, (11,))
-    on("B6", send_weights, 1, (14,))
-    on("B7", have_weights, 1, (14,))
-    on("B5", have_weights, 1, (13,))
-    on("B1", have_weights, 1, (0,))
+    on("A4", have_weights, 1, (1, 3))
+    on("A4", send_weights, 1, (5, 6))
+    on("A4", have_weights, 1, (2, 4))
+    on("A4", send_weights, 1, (7, 8))
+    on("B3", have_weights, 1, (7,))
+    on("B6", have_weights, 1, (5, 6))
+    on("B6", send_weights, 1, (9,))
+    on("B7", have_weights, 1, (9,))
+    on("B5", have_weights, 1, (8,))
 
     for j, phase in ((1, "A"), (0, "B")):
         for p in range(4):
             on(ORDER[AT[phase + str(2 * p + 1)] + 1], send_pair, j, p)
 
-    on("B2", send_diag, 1)
-    on("B6", send_free, 1, 1)
-    on("B6", send_free, 1, 2)
-    on("B7", send_rest, 1, 1)
-    on("B7", send_rest, 1, 2)
+    on("A3", send_diag, 1)
+    on("A5", send_free, 1, 1)
+    on("B3", send_free, 1, 2)
+    on("B3", send_rest, 1, 1)
+    on("B3", send_rest, 1, 2)
+    on("B4", send_free, 0, 1)
     on("B5", send_diag, 0)
-    on("C0", have_own, 1)
-    on("C0", add_up, 1, 0, 2)
-    on("C1", send_free, 0, 1)
-    on("C1", send_free, 0, 2)
-    on("C1", add_up, 1, 1, 3)
-    on("C2", middle, 1, 0, 2)
-    on("C3", send_rest, 0, 1)
-    on("C3", send_rest, 0, 2)
-    on("C3", middle, 1, 1, 3)
-    on("C4", ending, 1, 0, 2)
-    on("C5", ending, 1, 1, 3)
-
-    phases = {"A": phase_a, "B": phase_b, "C": phase_c}
+    on("D2", send_free, 0, 2)
+    on("C2", have_own, 1)
+    on("D2", add_up, 1, 0, 2)
+    on("C3", add_up, 1, 1, 3)
+    on("C5", middle, 1, 0)
+    on("C4", send_rest, 0, 1)
+    on("C4", send_rest, 0, 2)
+    on("D6", middle, 1, 2)
+    on("C7", have_own, 0)
+    on("C7", add_up, 0, 0, 2)
+    on("D7", add_up, 0, 1, 3)
+    on("D7", middle, 1, 1)
+    on("D7", ending, 1, 0)
+
+    phases = {"A": phase_a, "B": phase_b, "C": phase_c, "D": phase_d}
 
     def step(at, carry):
         q = jnp.int32(0)
         kind = jnp.int32(0)
         for index, name in enumerate(ORDER):
             q = jnp.where(at == index, int(name[1]), q)
-            kind = jnp.where(at == index, "ABC".index(name[0]), kind)
+            kind = jnp.where(at == index, "ABCD".index(name[0]), kind)
             if before[name]:
 
                 @pl.when(at == index)
@@ -533,7 +509,7 @@
                     for action in before[name]:
                         action()
 
-        for index, name in enumerate("ABC"):
+        for index, name in enumerate("ABCD"):
 
             @pl.when(kind == index)
             def _(name=name):
@@ -543,6 +519,9 @@
 
     lax.fori_loop(0, len(ORDER), step, 0)
 
+
+    middle(1, 3)
+    ending(1, 2)
 
     def together(state, carry):
         for at, (src, dst) in enumerate(((res_out, out_ref), (res_back, back_ref))):
@@ -553,16 +532,17 @@
         return carry
 
     lax.fori_loop(0, out_ref.shape[0], together, 0)
-    have_own(0)
-    add_up(0, 0, 2)
-    middle(0, 0, 2)
-    add_up(0, 1, 3)
-    ending(0, 0, 2)
-    middle(0, 1, 3)
-    ending(0, 1, 3)
+    middle(0, 0)
+    ending(1, 1)
+    middle(0, 2)
+    ending(1, 3)
+    middle(0, 1)
+    ending(0, 0)
+    middle(0, 3)
+    ending(0, 2, 1, 3)
     settle()
 
-    for at in range(15):
+    for at in range(10):
         give(0, at).wait_send()
         give(1, at).wait_send()
     for at in range(7):
@@ -572,23 +552,34 @@
             grad_copy(j, at).wait_send()
 
 
-def last_kernel(out_in, back_in, whole, out_ref, back_ref, grad_one, grad_two, bias_one, bias_two, sems):
+def last_kernel(
+    out_in, back_in, whole_in, out_ref, back_ref, grad_one, grad_two, bias_one, bias_two, boards, whole, grads, sems
+):
     channels = whole.shape[-1]
-    moves = [
-        pltpu.make_async_copy(src, dst, sems.at[at])
-        for at, (src, dst) in enumerate(((out_in, out_ref), (back_in, back_ref)))
+    chunks, quarter = whole.shape[1:3]
+
+    def move(src, dst, at):
+        return pltpu.make_async_copy(src, dst, sems.at[at])
+
+    loads = [move(whole_in, whole, 0), move(out_in, boards.at[0], 1), move(back_in, boards.at[1], 2)]
+    stores = [
+        move(boards.at[0], out_ref, 3), move(boards.at[1], back_ref, 4),
+        move(grads.at[0], grad_one.at[0], 5), move(grads.at[1], grad_two.at[0], 6),
     ]
-    for move in moves:
-        move.start()
-    chunks, quarter = whole.shape[1:3]
-    for j, (grad, bias) in enumerate(((grad_one, bias_one), (grad_two, bias_two))):
+    for load in loads:
+        load.start()
+    loads[0].wait()
+    for j, bias in enumerate((bias_one, bias_two)):
         stacked = jnp.concatenate([whole[j, at] for at in range(chunks)], axis=0).astype(jnp.float32)
         for tap in range(9):
             rows = slice(tap * channels, (tap + 1) * channels)
-            grad[0, rows, :] = stacked[rows].T
+            grads[j, rows, :] = stacked[rows].T
+        stores[2 + j].start()
+        loads[1 + j].wait()
+        stores[j].start()
         bias[...] = whole[j, chunks - 1, quarter - TAIL : quarter - TAIL + 8].astype(jnp.float32)[:1]
-    for move in moves:
-        move.wait()
+    for store in stores:
+        store.wait()
 
 
 def at_home(acts, cotangent, routes, w_first, w_second, b_first, b_second):
@@ -640,11 +631,11 @@
             board,
             board,
             pltpu.VMEM((owners, ROWS, channels), f32),
-            pltpu.VMEM((ROWS, channels), f32),
+            pltpu.VMEM((2, ROWS, channels), f32),
             results,
             results,
-            pltpu.VMEM((2, 4, rows_g, channels), f32),
-            pltpu.VMEM((2, 4, rows_g, channels), bf16),
+            pltpu.VMEM((2, owners, rows_g, channels), f32),
+            pltpu.VMEM((2, owners, rows_g, channels), bf16),
             pltpu.VMEM((2, 4, rows_g, channels), bf16),
             pltpu.VMEM((2, 4, rows_g, channels), bf16),
             pltpu.VMEM((2, 2, rows_g // 2, channels), bf16),
@@ -679,9 +670,14 @@
             shape((1, channels), f32),
             shape((1, channels), f32),
         ),
-        in_specs=[anywhere] * 2 + [vmem],
-        out_specs=(anywhere,) * 2 + (vmem,) * 4,
-        scratch_shapes=[sems((2,))],
+        in_specs=[anywhere] * 3,
+        out_specs=(anywhere,) * 4 + (vmem,) * 2,
+        scratch_shapes=[
+            pltpu.VMEM((2,) + x.shape, bf16),
+            pltpu.VMEM((2, 4, rows_g // 4, channels), bf16),
+            pltpu.VMEM((2, taps, channels), f32),
+            sems((7,)),
+        ],
         compiler_params=pltpu.CompilerParams(vmem_limit_bytes=60 * 1024 * 1024),
         cost_estimate=pl.CostEstimate(flops=0, bytes_accessed=5000000, transcendentals=0),
         name="last",

time: 130 us -> 78.8 us (0.61)
  Pallas kernels: 127 us -> 76.2 us
    pallas_call x1, Pallas kernels: 52.8 us -> 3.37 us  [at_home(): pl.pallas_call(last_kernel, out_shape=(shape(x.shape, bf16), shape(x.shap...]
    pallas_call x1, Pallas kernels: 74.5 us -> 72.8 us  [at_home(): pl.pallas_call(league_kernel, out_shape=(shape(x.shape, bf16), shape(x.sh...]
where the time goes in v4:
time: 78.8 us; the launch traced here: 78.6 us
  Pallas kernels  76.2 us (97%)
  other arithmetic  0.87 us (1%)
  local copies, waits for them, and re-layouts  0.84 us (1%)
    pallas_call x1, Pallas kernels, at_home(): pl.pallas_call(league_kernel, out_shape=(shape(x.shape, bf16), shape(x.sh...  72.8 us
    pallas_call x1, Pallas kernels, at_home(): pl.pallas_call(last_kernel, out_shape=(shape(x.shape, bf16), shape(x.shap...  3.37 us

profile of v4, /device:TPU:0, one launch (start us, length us, event | category | flops | bytes accessed | tf_op | source)
XLA Modules:
  0.0 78.6 jit_solution(8904411610514171675)
XLA Ops:
  0.6 0.0 copy-start
  0.6 0.7 copy-done
  1.3 0.1 copy.15
  1.4 0.1 reshape.43
  1.5 0.2 convert_reduce_fusion
  1.7 0.1 select_reduce_fusion
  1.8 0.6 pad_add_fusion.table
  2.4 72.8 %league.1 = (bf16[16,200,128]{2,1,0:T(8,128)(2,1)}, bf16[16,200,128]{2,1,0:T(8,128)(2,1)}, bf16[2,4,304,128]{3,2,1,0:T(8,128)(2,1)}) custom-call(s32[96]{0:T(128)} %pad_add_fusion.table, bf16[16,200,128]{2,1,0:T(8,128)(2,1)} %bitcast.12, bf16[16,200,128]{2,1,0:T(8,128)(2,1)} %bitcast.13, bf16[1,1152,128]{2,1,0:T(8,128)(2,1)} %w1_in.1, ...), custom_call_target="tpu_custom_call" | custom-call | flops 11324620800 | bytes 9000000 | tf_op jit(solution)/shard_map/league/pallas_call | solution.py:611
  75.2 3.4 %last.1 = (bf16[16,200,128]{2,1,0:T(8,128)(2,1)}, bf16[16,200,128]{2,1,0:T(8,128)(2,1)}, f32[1,1152,128]{2,1,0:T(8,128)}, f32[1,1152,128]{2,1,0:T(8,128)}, f32[1,128]{1,0:T(1,128)}, /*index=5*/f32[1,128]{1,0:T(1,128)}) custom-call(bf16[16,200,128]{2,1,0:T(8,128)(2,1)} %get-tuple-element.15.out_in, bf16[16,200,128]{2,1,0:T(8,128)(2,1)} %get-tuple-element.16.back_in, ...), custom_call_target="tpu_custom_call" | custom-call | bytes 5000000 | tf_op jit(solution)/shard_map/last/pallas_call | solution.py:663
  (2 shorter events, 0.0 us)
Async XLA Ops:
  0.6 0.7 copy-start

commit v5 on v4

--- a/solution.py
+++ b/solution.py
@@ -151,7 +151,8 @@
 ROWS = CELLS * SLOTS
 LINE = BOARD * SLOTS
 PLACES = SIDE * SIDE * SLOTS
-TAIL = 64
+TAIL = 16
+CHUNKS = 8
 MESH_ID = pl.DeviceIdType.MESH
 
 ORDER = (
@@ -171,19 +172,19 @@
 
 
 def league_kernel(
-    table, acts_in, cot_in, w1_in, w2_in, b1_in, b2_in,
-    out_ref, back_ref, whole,
-    acts_pair, cot_pair, pair, acts, cot, w1, w2, bs, xb, gb, hb, pb, slope, mix, res_out, res_back,
+    routes, acts_in, cot_in, w1_in, w2_in, b1_in, b2_in,
+    out_hbm, back_hbm, whole,
+    out_ref, back_ref, pair, acts, cot, w1, w2, bs, xb, gb, hb, pb, slope, mix, res_out, res_back,
     even, odd, paired, chips, diag, cross, total, split, outside, inside,
-    load_sems, w_send, w_recv, g_send, g_recv, z_send, z_recv,
+    lookup, table, load_sems, w_send, w_recv, g_send, g_recv, z_send, z_recv,
 ):
     f32, bf16 = jnp.float32, jnp.bfloat16
     channels = w1.shape[-1]
     taps = 9 * channels
     half_w = taps // 2
     rows_g = taps + TAIL
-    half_g = rows_g // 2
-    quarter = rows_g // 4
+    piece = taps // CHUNKS
+    half_g = taps // 2
     me = lax.axis_index("member")
     rep = lax.axis_index("rep")
     inner_plane = ((rep + 1) // 2) % 2 == 1
@@ -195,7 +196,7 @@
             (
                 (w1_in.at[0], w1.at[0]), (w2_in.at[0], w2.at[0]),
                 (b1_in, bs.at[0, pl.ds(0, 1), :]), (b2_in, bs.at[0, pl.ds(1, 1), :]),
-                (acts_in, acts_pair), (cot_in, cot_pair),
+                (acts_in, out_ref), (cot_in, back_ref),
             )
         )
     ]
@@ -256,25 +257,27 @@
         for at in ats:
             give_bias(at).wait_recv()
 
+    def span(c):
+        return c * piece, piece + (TAIL if c == CHUNKS - 1 else 0)
+
     def grad_copy(j, at):
         if at < 4:
             ends = (odd.at[j, 2 * at + 1], paired.at[j, at], "core")
         elif at < 6:
-            rows = pl.ds((at - 4) * half_g, half_g)
-            ends = (chips.at[j, 3, rows, :], diag.at[j, at - 4], "xy"[at - 4])
+            size = half_g + (at - 4) * TAIL
+            source = chips.at[j, 3, pl.ds((at - 4) * half_g, size), :]
+            ends = (source, diag.at[j, at - 4, pl.ds(0, size), :], "xy"[at - 4])
         else:
-            p, c = (at - 6) // 4, (at - 6) % 4
-            rows = pl.ds(c * quarter, quarter)
+            p, c = (at - 6) // CHUNKS, (at - 6) % CHUNKS
+            rows = pl.ds(*span(c))
             ends = (chips.at[j, p + 1, rows, :], cross.at[j, p, rows, :], "xy"[p])
-        return remote(ends[0], ends[1], g_send, g_recv, j * 16 + at, member(ends[2]))
+        return remote(ends[0], ends[1], g_send, g_recv, j * 24 + at, member(ends[2]))
 
     def rep_copy(j, stage, c):
-        src, dst, far = (
-            (split.at[j, c], outside.at[j, c], 1),
-            (split.at[j, c], inside.at[j, c], 3),
-            (whole.at[j, c], whole.at[j, c], 1),
-        )[stage]
-        return remote(src, dst, z_send, z_recv, (j * 3 + stage) * 4 + c, {"rep": rep ^ far})
+        src, dst, far = ((split, outside, 1), (split, inside, 3), (whole, whole, 1))[stage]
+        rows = pl.ds(*span(c))
+        at = (j * 3 + stage) * CHUNKS + c
+        return remote(src.at[j, rows, :], dst.at[j, rows, :], z_send, z_recv, at, {"rep": rep ^ far})
 
     def send_pair(j, p):
         grad_copy(j, p).start()
@@ -289,78 +292,96 @@
         grad_copy(j, p).wait_recv()
         rows = slice(0, half_g) if p == 1 else slice(half_g, rows_g)
         chips[j, p, rows] = (even[j, 2 * p, rows] + paired[j, p, rows].astype(f32)).astype(bf16)
-        for c in ((0, 1) if p == 1 else (2, 3)):
-            grad_copy(j, 6 + 4 * (p - 1) + c).start()
+        for c in (range(4) if p == 1 else range(4, 8)):
+            grad_copy(j, 6 + CHUNKS * (p - 1) + c).start()
 
     def send_rest(j, p):
         grad_copy(j, 6 - p).wait_recv()
         rows = slice(half_g, rows_g) if p == 1 else slice(0, half_g)
-        value = even[j, 2 * p, rows] + paired[j, p, rows].astype(f32) + diag[j, 2 - p].astype(f32)
+        value = even[j, 2 * p, rows] + paired[j, p, rows].astype(f32) + diag[j, 2 - p, : half_g + (2 - p) * TAIL].astype(f32)
         chips[j, p, rows] = value.astype(bf16)
-        for c in ((2, 3) if p == 1 else (0, 1)):
-            grad_copy(j, 6 + 4 * (p - 1) + c).start()
+        for c in (range(4, 8) if p == 1 else range(4)):
+            grad_copy(j, 6 + CHUNKS * (p - 1) + c).start()
 
     def have_own(j):
         grad_copy(j, 0).wait_recv()
 
     def add_up(j, *cs):
         for c in cs:
-            rows = slice(c * quarter, (c + 1) * quarter)
+            rows = pl.ds(*span(c))
             grad_copy(j, 6 + c).wait_recv()
-            grad_copy(j, 10 + c).wait_recv()
+            grad_copy(j, 6 + CHUNKS + c).wait_recv()
             value = even[j, 0, rows] + paired[j, 0, rows].astype(f32)
-            total[j, c] = value + cross[j, 0, rows].astype(f32) + cross[j, 1, rows].astype(f32)
+            total[j, rows] = value + cross[j, 0, rows].astype(f32) + cross[j, 1, rows].astype(f32)
 
             @pl.when(jnp.logical_not(inner_plane))
             def _():
-                split[j, c] = total[j, c].astype(bf16)
+                split[j, rows] = total[j, rows].astype(bf16)
                 rep_copy(j, 0, c).start()
 
     def middle(j, *cs):
         @pl.when(inner_plane)
         def _():
             for c in cs:
+                rows = pl.ds(*span(c))
                 rep_copy(j, 0, c).wait_recv()
-                split[j, c] = (total[j, c] + outside[j, c].astype(f32)).astype(bf16)
+                split[j, rows] = (total[j, rows] + outside[j, rows].astype(f32)).astype(bf16)
                 rep_copy(j, 1, c).start()
 
     def ending(j, *cs):
         @pl.when(inner_plane)
         def _():
             for c in cs:
+                rows = pl.ds(*span(c))
                 rep_copy(j, 1, c).wait_recv()
-                whole[j, c] = (split[j, c].astype(f32) + inside[j, c].astype(f32)).astype(bf16)
+                whole[j, rows] = (split[j, rows].astype(f32) + inside[j, rows].astype(f32)).astype(bf16)
                 rep_copy(j, 2, c).start()
 
     def settle():
         @pl.when(jnp.logical_not(inner_plane))
         def _():
             for j in range(2):
-                for c in range(4):
+                for c in range(CHUNKS):
                     rep_copy(j, 2, c).wait_recv()
                     rep_copy(j, 0, c).wait_send()
 
         @pl.when(inner_plane)
         def _():
             for j in range(2):
-                for c in range(4):
+                for c in range(CHUNKS):
                     rep_copy(j, 1, c).wait_send()
                     rep_copy(j, 2, c).wait_send()
 
     send_weights(0, (1, 3, 2, 4, 0))
     send_weights(1, (0,))
 
+    states = acts_in.shape[0]
+    count = 2 * states
+    lane = lax.broadcasted_iota(jnp.int32, (count, 128), 1)
+    line = lax.broadcasted_iota(jnp.int32, (count, 128), 0)
+    named = jnp.concatenate([routes[0:1, :], routes[1:2, :], jnp.full((1, 128 - count), -1, jnp.int32)], axis=1)
+    across = jnp.broadcast_to(named, (count, 128))
+    down = jnp.sum(jnp.where(lane == line, across, 0), axis=1, keepdims=True)
+    place = jnp.sum(jnp.where((line > lane) & (across == down), 1, 0), axis=1, keepdims=True)
+    position = jnp.bitwise_xor(down, me) * SLOTS + place
+    row = (line % states) * 2 + line // states
+    rows = jnp.sum(jnp.where(position == lane, row + 1, 0), axis=0, keepdims=True) - 1
+    positions = jnp.sum(jnp.where(lane == line + 8 * SLOTS, position, 0), axis=0, keepdims=True)
+    lookup[...] = jnp.where(lane[:1] < 8 * SLOTS, rows, positions)
+    fill = pltpu.make_async_copy(lookup, table, load_sems.at[6])
+    fill.start()
     for load in loads:
         load.wait()
 
     def apart(state, carry):
-        for at, (src, dst) in enumerate(((acts_pair, acts), (cot_pair, cot))):
+        for at, (src, dst) in enumerate(((out_ref, acts), (back_ref, cot))):
             pair[at] = src[state].astype(f32)
             for side in range(2):
                 dst[state * 2 + side] = pair[at, pl.ds(side, CELLS, stride=2), :].astype(bf16)
         return carry
 
-    lax.fori_loop(0, acts_pair.shape[0], apart, 0)
+    lax.fori_loop(0, out_ref.shape[0], apart, 0)
+    fill.wait()
 
     def patch(board, q):
         columns = []
@@ -390,8 +411,8 @@
 
     def gather(src, board, q, at):
         for slot in range(SLOTS):
-            row = table[q * SLOTS + slot]
-            value = src[jnp.maximum(row, 0)].astype(f32)
+            row = table[0, q * SLOTS + slot]
+            value = src[jnp.clip(row, 0, src.shape[0] - 1)].astype(f32)
             mix[at, pl.ds(slot, CELLS, stride=SLOTS), :] = jnp.where(row >= 0, value, 0.0)
         put(board, q, mix[at])
 
@@ -482,17 +503,17 @@
     on("B5", send_diag, 0)
     on("D2", send_free, 0, 2)
     on("C2", have_own, 1)
-    on("D2", add_up, 1, 0, 2)
-    on("C3", add_up, 1, 1, 3)
-    on("C5", middle, 1, 0)
+    on("D2", add_up, 1, 0, 4, 1, 5)
+    on("C3", add_up, 1, 2, 6, 3, 7)
+    on("C5", middle, 1, 0, 4)
     on("C4", send_rest, 0, 1)
     on("C4", send_rest, 0, 2)
-    on("D6", middle, 1, 2)
+    on("D6", middle, 1, 1, 5)
     on("C7", have_own, 0)
-    on("C7", add_up, 0, 0, 2)
-    on("D7", add_up, 0, 1, 3)
-    on("D7", middle, 1, 1)
-    on("D7", ending, 1, 0)
+    on("C7", add_up, 0, 0, 4, 1, 5)
+    on("D7", add_up, 0, 2, 6, 3, 7)
+    on("D7", middle, 1, 2, 6)
+    on("D7", ending, 1, 0, 4)
 
     phases = {"A": phase_a, "B": phase_b, "C": phase_c, "D": phase_d}
 
@@ -520,27 +541,40 @@
     lax.fori_loop(0, len(ORDER), step, 0)
 
 
-    middle(1, 3)
-    ending(1, 2)
+    middle(1, 3, 7)
+    ending(1, 1, 5)
 
     def together(state, carry):
         for at, (src, dst) in enumerate(((res_out, out_ref), (res_back, back_ref))):
             for side in range(2):
-                row = table[8 * SLOTS + state * 2 + side]
+                row = jnp.clip(table[0, 8 * SLOTS + side * out_ref.shape[0] + state], 0, src.shape[0] - 1)
                 pair[at, pl.ds(side, CELLS, stride=2), :] = src[row].astype(f32)
             dst[state] = pair[at].astype(bf16)
         return carry
 
     lax.fori_loop(0, out_ref.shape[0], together, 0)
-    middle(0, 0)
-    ending(1, 1)
+    stores = [
+        pltpu.make_async_copy(src, dst, load_sems.at[at])
+        for at, (src, dst) in enumerate(((out_ref, out_hbm), (back_ref, back_hbm)))
+    ]
+    for store in stores:
+        store.start()
+    middle(0, 0, 4)
+    ending(1, 2, 6)
+    middle(0, 1, 5)
+    ending(1, 3, 7)
+    ending(0, 0)
     middle(0, 2)
-    ending(1, 3)
-    middle(0, 1)
-    ending(0, 0)
+    ending(0, 4)
+    middle(0, 6)
+    ending(0, 1)
     middle(0, 3)
-    ending(0, 2, 1, 3)
+    ending(0, 5)
+    middle(0, 7)
+    ending(0, 2, 6, 3, 7)
     settle()
+    for store in stores:
+        store.wait()
 
     for at in range(10):
         give(0, at).wait_send()
@@ -548,7 +582,7 @@
     for at in range(7):
         give_bias(at).wait_send()
     for j in range(2):
-        for at in range(14):
+        for at in range(6 + 2 * CHUNKS):
             grad_copy(j, at).wait_send()
 
 
@@ -556,7 +590,7 @@
     out_in, back_in, whole_in, out_ref, back_ref, grad_one, grad_two, bias_one, bias_two, boards, whole, grads, sems
 ):
     channels = whole.shape[-1]
-    chunks, quarter = whole.shape[1:3]
+    taps = grads.shape[1]
 
     def move(src, dst, at):
         return pltpu.make_async_copy(src, dst, sems.at[at])
@@ -570,14 +604,14 @@
         load.start()
     loads[0].wait()
     for j, bias in enumerate((bias_one, bias_two)):
-        stacked = jnp.concatenate([whole[j, at] for at in range(chunks)], axis=0).astype(jnp.float32)
+        stacked = whole[j].astype(jnp.float32)
         for tap in range(9):
             rows = slice(tap * channels, (tap + 1) * channels)
             grads[j, rows, :] = stacked[rows].T
         stores[2 + j].start()
         loads[1 + j].wait()
         stores[j].start()
-        bias[...] = whole[j, chunks - 1, quarter - TAIL : quarter - TAIL + 8].astype(jnp.float32)[:1]
+        bias[...] = whole[j, taps : taps + 8].astype(jnp.float32)[:1]
     for store in stores:
         store.wait()
 
@@ -588,15 +622,8 @@
     taps = 9 * channels
     rows_g = taps + TAIL
     f32, bf16 = jnp.float32, jnp.bfloat16
-    me = lax.axis_index("member")
-    ids = routes.reshape(-1)
-    count = ids.shape[0]
-    order = jnp.arange(count, dtype=jnp.int32)
-    place = jnp.sum(((order[:, None] > order[None, :]) & (ids[:, None] == ids[None, :])).astype(jnp.int32), axis=1)
-    position = (ids ^ me) * SLOTS + place
-    hit = position[None, :] == jnp.arange(owners * SLOTS, dtype=jnp.int32)[:, None]
-    rows = jnp.sum(jnp.where(hit, order[None, :] + 1, 0), axis=1) - 1
-    table = jnp.concatenate([rows, position])
+    count = 2 * routes.shape[0]
+
     def paired(values):
         return jnp.swapaxes(values, 1, 2).reshape(values.shape[0], 2 * values.shape[2], channels)
 
@@ -613,10 +640,10 @@
         out_shape=(
             shape(x.shape, bf16),
             shape(x.shape, bf16),
-            shape((2, 4, rows_g // 4, channels), bf16),
+            shape((2, rows_g, channels), bf16),
         ),
-        in_specs=[pl.BlockSpec(memory_space=pltpu.SMEM)] + [anywhere] * 6,
-        out_specs=(vmem,) * 3,
+        in_specs=[vmem] + [anywhere] * 6,
+        out_specs=(anywhere, anywhere, vmem),
         scratch_shapes=[
             pltpu.VMEM(x.shape, bf16),
             pltpu.VMEM(x.shape, bf16),
@@ -638,19 +665,21 @@
             pltpu.VMEM((2, owners, rows_g, channels), bf16),
             pltpu.VMEM((2, 4, rows_g, channels), bf16),
             pltpu.VMEM((2, 4, rows_g, channels), bf16),
-            pltpu.VMEM((2, 2, rows_g // 2, channels), bf16),
+            pltpu.VMEM((2, 2, taps // 2 + TAIL, channels), bf16),
             pltpu.VMEM((2, 2, rows_g, channels), bf16),
-            pltpu.VMEM((2, 4, rows_g // 4, channels), f32),
-            pltpu.VMEM((2, 4, rows_g // 4, channels), bf16),
-            pltpu.VMEM((2, 4, rows_g // 4, channels), bf16),
-            pltpu.VMEM((2, 4, rows_g // 4, channels), bf16),
-            sems((6,)),
+            pltpu.VMEM((2, rows_g, channels), f32),
+            pltpu.VMEM((2, rows_g, channels), bf16),
+            pltpu.VMEM((2, rows_g, channels), bf16),
+            pltpu.VMEM((2, rows_g, channels), bf16),
+            pltpu.VMEM((1, 128), jnp.int32),
+            pltpu.SMEM((1, 128), jnp.int32),
+            sems((7,)),
             sems((40,)),
             sems((40,)),
-            sems((32,)),
-            sems((32,)),
-            sems((24,)),
-            sems((24,)),
+            sems((48,)),
+            sems((48,)),
+            sems((48,)),
+            sems((48,)),
         ],
         compiler_params=pltpu.CompilerParams(
             collective_id=0, has_side_effects=True, vmem_limit_bytes=60 * 1024 * 1024
@@ -659,7 +688,7 @@
             flops=12 * owners * ROWS * taps * channels, bytes_accessed=9000000, transcendentals=owners * ROWS * channels
         ),
         name="league",
-    )(table, x, g, w_first, w_second, b_first, b_second)
+    )(routes.T, x, g, w_first, w_second, b_first, b_second)
     done = pl.pallas_call(
         last_kernel,
         out_shape=(
@@ -674,7 +703,7 @@
         out_specs=(anywhere,) * 4 + (vmem,) * 2,
         scratch_shapes=[
             pltpu.VMEM((2,) + x.shape, bf16),
-            pltpu.VMEM((2, 4, rows_g // 4, channels), bf16),
+            pltpu.VMEM((2, rows_g, channels), bf16),
             pltpu.VMEM((2, taps, channels), f32),
             sems((7,)),
         ],

time: 78.8 us -> 76.3 us (0.968)
  other arithmetic: 0.87 us -> 0 us
  local copies, waits for them, and re-layouts: 0.84 us -> 0 us
where the time goes in v5:
time: 76.3 us; the launch traced here: 76.1 us
  Pallas kernels  75.5 us (99%)
    pallas_call x1, Pallas kernels, at_home(): pl.pallas_call(league_kernel, out_shape=(shape(x.shape, bf16), shape(x.sh...  72.1 us
    pallas_call x1, Pallas kernels, at_home(): pl.pallas_call(last_kernel, out_shape=(shape(x.shape, bf16), shape(x.shap...  3.36 us

profile of v5, /device:TPU:0, one launch (start us, length us, event | category | flops | bytes accessed | tf_op | source)
XLA Modules:
  0.0 76.1 jit_solution(5545641380476827369)
XLA Ops:
  0.6 72.1 %league.1 = (bf16[16,200,128]{2,1,0:T(8,128)(2,1)}, bf16[16,200,128]{2,1,0:T(8,128)(2,1)}, bf16[2,1168,128]{2,1,0:T(8,128)(2,1)}) custom-call(s32[2,16]{1,0:T(2,128)} %bitcast.17, bf16[16,200,128]{2,1,0:T(8,128)(2,1)} %bitcast.13, bf16[16,200,128]{2,1,0:T(8,128)(2,1)} %bitcast.14, bf16[1,1152,128]{2,1,0:T(8,128)(2,1)} %w1_in.1, bf16[1,1152,128]{2,1,0:T(8,128)(2,1)} %w2_in.1, ...), custom_call_target="tpu_custom_call" | custom-call | flops 11324620800 | bytes 9000000 | tf_op jit(solution)/shard_map/league/pallas_call | solution.py:638
  72.8 3.4 %last.1 = (bf16[16,200,128]{2,1,0:T(8,128)(2,1)}, bf16[16,200,128]{2,1,0:T(8,128)(2,1)}, f32[1,1152,128]{2,1,0:T(8,128)}, f32[1,1152,128]{2,1,0:T(8,128)}, f32[1,128]{1,0:T(1,128)}, /*index=5*/f32[1,128]{1,0:T(1,128)}) custom-call(bf16[16,200,128]{2,1,0:T(8,128)(2,1)} %get-tuple-element.15.out_in, bf16[16,200,128]{2,1,0:T(8,128)(2,1)} %get-tuple-element.16.back_in, ...), custom_call_target="tpu_custom_call" | custom-call | bytes 5000000 | tf_op jit(solution)/shard_map/last/pallas_call | solution.py:692

commit v6 on v5

--- a/solution.py
+++ b/solution.py
@@ -495,7 +495,7 @@
             on(ORDER[AT[phase + str(2 * p + 1)] + 1], send_pair, j, p)
 
     on("A3", send_diag, 1)
-    on("A5", send_free, 1, 1)
+    on("B2", send_free, 1, 1)
     on("B3", send_free, 1, 2)
     on("B3", send_rest, 1, 1)
     on("B3", send_rest, 1, 2)

time: 76.3 us -> 76 us (level)
  no operation moved by 1% of the time
where the time goes in v6:
time: 76 us; the launch traced here: 75.8 us
  Pallas kernels  75.2 us (99%)
    pallas_call x1, Pallas kernels, at_home(): pl.pallas_call(league_kernel, out_shape=(shape(x.shape, bf16), shape(x.sh...  71.8 us
    pallas_call x1, Pallas kernels, at_home(): pl.pallas_call(last_kernel, out_shape=(shape(x.shape, bf16), shape(x.shap...  3.36 us

profile of v6, /device:TPU:0, one launch (start us, length us, event | category | flops | bytes accessed | tf_op | source)
XLA Modules:
  0.0 75.8 jit_solution(13123038786865325709)
XLA Ops:
  0.6 71.8 %league.1 = (bf16[16,200,128]{2,1,0:T(8,128)(2,1)}, bf16[16,200,128]{2,1,0:T(8,128)(2,1)}, bf16[2,1168,128]{2,1,0:T(8,128)(2,1)}) custom-call(s32[2,16]{1,0:T(2,128)} %bitcast.17, bf16[16,200,128]{2,1,0:T(8,128)(2,1)} %bitcast.13, bf16[16,200,128]{2,1,0:T(8,128)(2,1)} %bitcast.14, bf16[1,1152,128]{2,1,0:T(8,128)(2,1)} %w1_in.1, bf16[1,1152,128]{2,1,0:T(8,128)(2,1)} %w2_in.1, ...), custom_call_target="tpu_custom_call" | custom-call | flops 11324620800 | bytes 9000000 | tf_op jit(solution)/shard_map/league/pallas_call | solution.py:638
  72.4 3.4 %last.1 = (bf16[16,200,128]{2,1,0:T(8,128)(2,1)}, bf16[16,200,128]{2,1,0:T(8,128)(2,1)}, f32[1,1152,128]{2,1,0:T(8,128)}, f32[1,1152,128]{2,1,0:T(8,128)}, f32[1,128]{1,0:T(1,128)}, /*index=5*/f32[1,128]{1,0:T(1,128)}) custom-call(bf16[16,200,128]{2,1,0:T(8,128)(2,1)} %get-tuple-element.15.out_in, bf16[16,200,128]{2,1,0:T(8,128)(2,1)} %get-tuple-element.16.back_in, ...), custom_call_target="tpu_custom_call" | custom-call | bytes 5000000 | tf_op jit(solution)/shard_map/last/pallas_call | solution.py:692

commit v7 on v6

--- a/solution.py
+++ b/solution.py
@@ -595,21 +595,24 @@
     def move(src, dst, at):
         return pltpu.make_async_copy(src, dst, sems.at[at])
 
-    loads = [move(whole_in, whole, 0), move(out_in, boards.at[0], 1), move(back_in, boards.at[1], 2)]
+    loads = [
+        move(whole_in.at[0], whole.at[0], 0), move(out_in, boards.at[0], 1),
+        move(whole_in.at[1], whole.at[1], 7), move(back_in, boards.at[1], 2),
+    ]
     stores = [
         move(boards.at[0], out_ref, 3), move(boards.at[1], back_ref, 4),
         move(grads.at[0], grad_one.at[0], 5), move(grads.at[1], grad_two.at[0], 6),
     ]
     for load in loads:
         load.start()
-    loads[0].wait()
     for j, bias in enumerate((bias_one, bias_two)):
+        loads[2 * j].wait()
         stacked = whole[j].astype(jnp.float32)
         for tap in range(9):
             rows = slice(tap * channels, (tap + 1) * channels)
             grads[j, rows, :] = stacked[rows].T
         stores[2 + j].start()
-        loads[1 + j].wait()
+        loads[2 * j + 1].wait()
         stores[j].start()
         bias[...] = whole[j, taps : taps + 8].astype(jnp.float32)[:1]
     for store in stores:
@@ -705,7 +708,7 @@
             pltpu.VMEM((2,) + x.shape, bf16),
             pltpu.VMEM((2, rows_g, channels), bf16),
             pltpu.VMEM((2, taps, channels), f32),
-            sems((7,)),
+            sems((8,)),
         ],
         compiler_params=pltpu.CompilerParams(vmem_limit_bytes=60 * 1024 * 1024),
         cost_estimate=pl.CostEstimate(flops=0, bytes_accessed=5000000, transcendentals=0),

time: 76 us -> 75.9 us (level)
  no operation moved by 1% of the time
where the time goes in v7:
time: 75.9 us; the launch traced here: 75.7 us
  Pallas kernels  75 us (99%)
    pallas_call x1, Pallas kernels, at_home(): pl.pallas_call(league_kernel, out_shape=(shape(x.shape, bf16), shape(x.sh...  71.8 us
    pallas_call x1, Pallas kernels, at_home(): pl.pallas_call(last_kernel, out_shape=(shape(x.shape, bf16), shape(x.shap...  3.27 us

profile of v7, /device:TPU:0, one launch (start us, length us, event | category | flops | bytes accessed | tf_op | source)
XLA Modules:
  0.0 75.7 jit_solution(14869836071527687569)
XLA Ops:
  0.6 71.8 %league.1 = (bf16[16,200,128]{2,1,0:T(8,128)(2,1)}, bf16[16,200,128]{2,1,0:T(8,128)(2,1)}, bf16[2,1168,128]{2,1,0:T(8,128)(2,1)}) custom-call(s32[2,16]{1,0:T(2,128)} %bitcast.17, bf16[16,200,128]{2,1,0:T(8,128)(2,1)} %bitcast.13, bf16[16,200,128]{2,1,0:T(8,128)(2,1)} %bitcast.14, bf16[1,1152,128]{2,1,0:T(8,128)(2,1)} %w1_in.1, bf16[1,1152,128]{2,1,0:T(8,128)(2,1)} %w2_in.1, ...), custom_call_target="tpu_custom_call" | custom-call | flops 11324620800 | bytes 9000000 | tf_op jit(solution)/shard_map/league/pallas_call | solution.py:641
  72.4 3.3 %last.1 = (bf16[16,200,128]{2,1,0:T(8,128)(2,1)}, bf16[16,200,128]{2,1,0:T(8,128)(2,1)}, f32[1,1152,128]{2,1,0:T(8,128)}, f32[1,1152,128]{2,1,0:T(8,128)}, f32[1,128]{1,0:T(1,128)}, /*index=5*/f32[1,128]{1,0:T(1,128)}) custom-call(bf16[16,200,128]{2,1,0:T(8,128)(2,1)} %get-tuple-element.15.out_in, bf16[16,200,128]{2,1,0:T(8,128)(2,1)} %get-tuple-element.16.back_in, ...), custom_call_target="tpu_custom_call" | custom-call | bytes 5000000 | tf_op jit(solution)/shard_map/last/pallas_call | solution.py:695

commit v8 on v6

--- a/solution.py
+++ b/solution.py
@@ -497,8 +497,8 @@
     on("A3", send_diag, 1)
     on("B2", send_free, 1, 1)
     on("B3", send_free, 1, 2)
-    on("B3", send_rest, 1, 1)
-    on("B3", send_rest, 1, 2)
+    on("B6", send_rest, 1, 1)
+    on("B6", send_rest, 1, 2)
     on("B4", send_free, 0, 1)
     on("B5", send_diag, 0)
     on("D2", send_free, 0, 2)

time: 76 us -> 75.9 us (level)
  no operation moved by 1% of the time
where the time goes in v8:
time: 75.9 us; the launch traced here: 75.7 us
  Pallas kernels  75.1 us (99%)
    pallas_call x1, Pallas kernels, at_home(): pl.pallas_call(league_kernel, out_shape=(shape(x.shape, bf16), shape(x.sh...  71.7 us
    pallas_call x1, Pallas kernels, at_home(): pl.pallas_call(last_kernel, out_shape=(shape(x.shape, bf16), shape(x.shap...  3.36 us

profile of v8, /device:TPU:0, one launch (start us, length us, event | category | flops | bytes accessed | tf_op | source)
XLA Modules:
  0.0 75.7 jit_solution(6178585298269477893)
XLA Ops:
  0.6 71.7 %league.1 = (bf16[16,200,128]{2,1,0:T(8,128)(2,1)}, bf16[16,200,128]{2,1,0:T(8,128)(2,1)}, bf16[2,1168,128]{2,1,0:T(8,128)(2,1)}) custom-call(s32[2,16]{1,0:T(2,128)} %bitcast.17, bf16[16,200,128]{2,1,0:T(8,128)(2,1)} %bitcast.13, bf16[16,200,128]{2,1,0:T(8,128)(2,1)} %bitcast.14, bf16[1,1152,128]{2,1,0:T(8,128)(2,1)} %w1_in.1, bf16[1,1152,128]{2,1,0:T(8,128)(2,1)} %w2_in.1, ...), custom_call_target="tpu_custom_call" | custom-call | flops 11324620800 | bytes 9000000 | tf_op jit(solution)/shard_map/league/pallas_call | solution.py:638
  72.4 3.4 %last.1 = (bf16[16,200,128]{2,1,0:T(8,128)(2,1)}, bf16[16,200,128]{2,1,0:T(8,128)(2,1)}, f32[1,1152,128]{2,1,0:T(8,128)}, f32[1,1152,128]{2,1,0:T(8,128)}, f32[1,128]{1,0:T(1,128)}, /*index=5*/f32[1,128]{1,0:T(1,128)}) custom-call(bf16[16,200,128]{2,1,0:T(8,128)(2,1)} %get-tuple-element.15.out_in, bf16[16,200,128]{2,1,0:T(8,128)(2,1)} %get-tuple-element.16.back_in, ...), custom_call_target="tpu_custom_call" | custom-call | bytes 5000000 | tf_op jit(solution)/shard_map/last/pallas_call | solution.py:692
